TPU v7x, 32 devices: a whole 2x2x4 slice. The times are simulated.
32 devices in a mesh: tensor: 4 (over z), row: 2 (over core), col: 4 (over y, x).
Axes of the slice: x: 2, y: 2, z: 4, core: 2. Of those that a mesh axis runs over, the one named last changes fastest.
Arguments:
- features: bfloat16 [1024, 6144], P(('row', 'col'), 'tensor'), may hold values from -8 to 8
- w_proj: bfloat16 [6144, 1024], P('tensor'), may hold values from -0.078125 to 0.078125
- flags: int32 [1024], P(('row', 'col')), may hold values 0 or 1
- rates: float32 [5], replicated, may hold values from 0.25 to 4
Outputs:
- feature_grad: bfloat16 [1024, 6144], P(('row', 'col'), 'tensor')
All inputs are finite; a program needn't handle non-finite values. No bound on the sum of `flags` on one device may be relied on, other than what follows from the above.
Results may differ from a plain program's by a relative error of at most 0.029.
Values may be sent and summed in bfloat16 or wider, within the bound.
A program may use at most 64 MiB of HBM per device.

v0:
```python
import jax
import jax.numpy as jnp
from jax import lax
from jax.sharding import PartitionSpec as P


def tensor_sum(value):
    return lax.psum(value.astype(jnp.bfloat16), "tensor").astype(jnp.float32)


def shards(features, w_proj, flags, rates):
    group = features.shape[0]
    width = w_proj.shape[1]
    n_tensor = lax.axis_size("tensor")
    quarter = group // n_tensor
    tpos = lax.axis_index("tensor")
    signs = (1 - 2 * flags).astype(jnp.bfloat16)
    own_s = lax.dynamic_slice_in_dim(signs, tpos * quarter, quarter, 0)
    proj_full = tensor_sum(jnp.dot(features, w_proj, preferred_element_type=jnp.float32)).astype(
        jnp.bfloat16
    )
    own_z = lax.dynamic_slice_in_dim(proj_full, tpos * quarter, quarter, 0)
    row_z, row_s = (
        lax.all_gather(proj_full, "row", axis=0, tiled=True),
        lax.all_gather(signs, "row", axis=0, tiled=True),
    )
    col_z, col_s = (
        lax.all_gather(own_z, "col", axis=0, tiled=True),
        lax.all_gather(own_s, "col", axis=0, tiled=True),
    )
    row_norm = jnp.sum(jnp.square(row_z.astype(jnp.float32)), axis=1)
    col_norm = jnp.sum(jnp.square(col_z.astype(jnp.float32)), axis=1)
    cross = lax.dot_general(
        row_z, col_z, (((1,), (1,)), ((), ())), preferred_element_type=jnp.float32
    )
    dist = jnp.maximum(row_norm[:, None] + col_norm[None, :] - 2.0 * cross, 0.0) / width
    kernel = jnp.zeros_like(dist)
    for band in range(rates.shape[0]):
        kernel = kernel + rates[band] * jnp.exp(-rates[band] * dist)
    mixed = (
        -16.0
        / width
        * row_s.astype(jnp.float32)[:, None]
        * col_s.astype(jnp.float32)[None, :]
        * kernel
    )
    rounded = mixed.astype(jnp.bfloat16)
    row_total = jnp.sum(mixed, axis=1)
    col_total = jnp.sum(mixed, axis=0)
    block = rounded
    lead = col_total
    own_rows = col_z
    other = lax.dot_general(
        block, row_z, (((0,), (0,)), ((), ())), preferred_element_type=jnp.float32
    )
    col_part = lax.psum_scatter(
        (lead[:, None] * own_rows.astype(jnp.float32) - other).astype(jnp.bfloat16),
        "col",
        scatter_dimension=0,
        tiled=True,
    ).astype(jnp.float32)
    block = rounded
    lead = row_total
    own_rows = row_z
    row_part = lax.psum_scatter(
        (
            lead[:, None] * own_rows.astype(jnp.float32)
            - jnp.dot(block, col_z, preferred_element_type=jnp.float32)
        ).astype(jnp.bfloat16),
        "row",
        scatter_dimension=0,
        tiled=True,
    ).astype(jnp.float32)
    placed = lax.dynamic_update_slice_in_dim(
        jnp.zeros((group, width), jnp.float32), col_part, tpos * quarter, 0
    )
    grad_z = tensor_sum(row_part + placed).astype(jnp.bfloat16)
    result = lax.dot_general(
        grad_z, w_proj, (((1,), (1,)), ((), ())), preferred_element_type=jnp.float32
    )
    return result.astype(jnp.bfloat16)


def solution(mesh):
    in_specs = (P(("row", "col"), "tensor"), P("tensor", None), P(("row", "col")), P())
    out_specs = P(("row", "col"), "tensor")
    return jax.shard_map(shards, mesh=mesh, in_specs=in_specs, out_specs=out_specs, check_vma=False)
```

profile of v0, /device:TPU:1, one launch (start us, length us, event | category | flops | bytes accessed | tf_op | source)
XLA Modules:
  0.0 147.5 jit_solution(212119660292656078)
XLA Ops:
  6.6 1.9 %copy-done = bf16[1536,1024]{1,0:T(8,128)(2,1)S(1)} copy-done((bf16[1536,1024]{1,0:T(8,128)(2,1)S(1)}, bf16[1536,1024]{1,0:T(8,128)(2,1)}, u32[]{:S(2)}) %copy-start) | copy-done | bytes 3145752
  8.5 2.3 %convolution_convert_fusion.1 = bf16[128,1024]{1,0:T(8,128)(2,1)} fusion(bf16[128,1536]{1,0:T(8,128)(2,1)} %param.4, bf16[1536,1024]{1,0:T(8,128)(2,1)S(1)} %copy-done), kind=kOutput, calls=%fused_computation.6 | convolution fusion | flops 402784256 | bytes 3801088 | tf_op jit(solution)/shard_map/dot_general | solution.py:19
  10.8 0.7 fusion.10
  11.5 0.6 dynamic-slice.1
  12.8 0.1 dynamic_slice.6
  12.9 0.2 dynamic-update-slice.1
  13.1 8.7 %all-reduce = bf16[128]{0:T(256)(128)(2,1)S(1)} all-reduce(bf16[128]{0:T(256)(128)(2,1)S(1)} %dynamic-update-slice.1), channel_id=1, replica_groups=mesh['tensor'=4,'row'=2,'col'=4] {'col'}, use_global_device_ids=true, to_apply=%add | all-reduce | flops 128 | bytes 512
  24.8 4.2 %all-gather = bf16[2,1,128]{2,1,0:T(2,128)(2,1)S(1)} all-gather(bf16[1,1,128]{2,1,0:T(2,128)(2,1)S(1)} %get-tuple-element.7), channel_id=1, replica_groups=mesh['tensor'=4,'row'=2,'col'=4] {'row'}, dimensions={0}, use_global_device_ids=true | all-gather | bytes 768 | tf_op jit(solution)/shard_map/all_gather | solution.py:25
  29.0 18.0 %all-reduce.4.cloned.1.call-done = bf16[128,1024]{1,0:T(8,128)(2,1)} async-done(((bf16[128,1024]{1,0:T(8,128)(2,1)}), bf16[128,1024]{1,0:T(8,128)(2,1)}) %all-reduce.4.cloned.1.call-update) | async-done | bytes 262160 | tf_op jit(solution)/shard_map/psum | solution.py:8
  47.0 0.8 constant_dynamic-slice_fusion
  47.8 6.9 %all_gather.15 = bf16[128,1024]{1,0:T(8,128)(2,1)S(1)} all-gather(bf16[32,1024]{1,0:T(8,128)(2,1)S(1)} %constant_dynamic-slice_fusion), channel_id=1, replica_groups=mesh['tensor'=4,'row'=2,'col'=4] {'col'}, dimensions={0}, use_global_device_ids=true | all-gather | bytes 327680 | tf_op jit(solution)/shard_map/all_gather | solution.py:28
  54.7 0.1 fusion.5
  54.9 6.4 %all_gather.14 = bf16[256,1024]{1,0:T(8,128)(2,1)S(1)} all-gather(bf16[128,1024]{1,0:T(8,128)(2,1)} %all-reduce.4.cloned.1.call-done), channel_id=1, replica_groups=mesh['tensor'=4,'row'=2,'col'=4] {'row'}, dimensions={0}, use_global_device_ids=true | all-gather | bytes 786432 | tf_op jit(solution)/shard_map/all_gather | solution.py:24
  61.3 0.2 fusion.4
  61.5 3.5 %fusion.9 = (f32[128]{0:T(128)S(1)}, f32[256]{0:T(256)S(1)}, bf16[256,128]{1,0:T(8,128)(2,1)S(1)}) fusion(f32[]{:T(128)S(6)} %mul.157, f32[]{:T(128)} %bitcast.7, f32[]{:T(128)S(6)} %mul.152, f32[]{:T(128)} %bitcast.6, f32[]{:T(128)S(6)} %mul.147, f32[]{:T(128)} %bitcast.5, f32[]{:T(128)S(6)} %mul.142, f32[]{:T(128)} %bitcast.4, f32[]{:T(128)S(6)} %mul.137, ...), kind=kOutput, calls=%fused_computation.23 | convolution fusion | flops 67862144 | bytes 856616 | tf_op jit(solution)/shard_map/dot_general | solution.py:33
  65.0 1.1 fusion
  66.2 2.0 %fusion.1 = bf16[128,1024]{1,0:T(8,128)(2,1)} fusion(bf16[256,1024]{1,0:T(8,128)(2,1)} %copy-done.1, bf16[128,1024]{1,0:T(8,128)(2,1)S(1)} %all_gather.15, f32[128]{0:T(128)S(1)} %get-tuple-element.5, bf16[256,128]{1,0:T(8,128)(2,1)S(1)} %get-tuple-element.14), kind=kOutput, calls=%fused_computation.7 | convolution fusion | flops 67633152 | bytes 1114624 | tf_op jit(solution)/shard_map/dot_general | solution.py:53
  68.3 4.7 %reduce-scatter.3.cloned.1.call-done = bf16[128,1024]{1,0:T(8,128)(2,1)} async-done(((bf16[256,1024]{1,0:T(8,128)(2,1)}), bf16[128,1024]{1,0:T(8,128)(2,1)}) %reduce-scatter.3.cloned.1.call-update) | async-done | bytes 262160 | tf_op jit(solution)/shard_map/reduce_scatter | solution.py:65
  72.9 1.8 %convert_element_type.55 = f32[128,1024]{1,0:T(8,128)} convert(bf16[128,1024]{1,0:T(8,128)(2,1)} %reduce-scatter.3.cloned.1.call-done) | non-fusion elementwise | flops 131072 | bytes 786432 | tf_op jit(solution)/shard_map/convert_element_type | solution.py:73
  74.7 25.4 %reduce-scatter.5.cloned.1.call-done = bf16[32,1024]{1,0:T(8,128)(2,1)} async-done(((bf16[128,1024]{1,0:T(8,128)(2,1)}), bf16[32,1024]{1,0:T(8,128)(2,1)}) %reduce-scatter.5.cloned.1.call-update) | async-done | bytes 65552 | tf_op jit(solution)/shard_map/reduce_scatter | solution.py:56
  100.1 1.6 %add_dynamic-update-slice_fusion = f32[128,1024]{1,0:T(8,128)} fusion(f32[128,1024]{1,0:T(8,128)} %convert_element_type.55, s32[]{:T(128)S(6)} %select_n.2, bf16[32,1024]{1,0:T(8,128)(2,1)} %reduce-scatter.5.cloned.1.call-done), kind=kLoop, calls=%fused_computation.15 | loop fusion | flops 65536 | bytes 327684 | tf_op jit(solution)/shard_map/add | solution.py:77
  101.7 1.8 %convert_element_type.59 = bf16[128,1024]{1,0:T(8,128)(2,1)} convert(f32[128,1024]{1,0:T(8,128)} %add_dynamic-update-slice_fusion) | non-fusion elementwise | flops 131072 | bytes 786432 | tf_op jit(solution)/shard_map/convert_element_type | solution.py:8
  103.5 34.6 %all-reduce.6.cloned.1.call-done = bf16[128,1024]{1,0:T(8,128)(2,1)} async-done(((bf16[128,1024]{1,0:T(8,128)(2,1)}), bf16[128,1024]{1,0:T(8,128)(2,1)}) %all-reduce.6.cloned.1.call-update) | async-done | bytes 262160 | tf_op jit(solution)/shard_map/psum | solution.py:8
  138.1 2.9 %convolution_convert_fusion = bf16[128,1536]{1,0:T(8,128)(2,1)} fusion(bf16[128,1024]{1,0:T(8,128)(2,1)} %all-reduce.6.cloned.1.call-done, bf16[1536,1024]{1,0:T(8,128)(2,1)S(1)} %copy-done), kind=kOutput, calls=%fused_computation | convolution fusion | flops 402849792 | bytes 3801088 | tf_op jit(solution)/shard_map/dot_general | solution.py:78
  (21 shorter events, 0.3 us)
Async XLA Ops:
  6.5 1.9 %copy-start = (bf16[1536,1024]{1,0:T(8,128)(2,1)S(1)}, bf16[1536,1024]{1,0:T(8,128)(2,1)}, u32[]{:S(2)}) copy-start(bf16[1536,1024]{1,0:T(8,128)(2,1)} %param.5) | copy-start | bytes 9437188
  6.5 5.0 %copy-start.4 = (u32[32]{0:T(128)S(1)}, u32[32]{0:T(128)}, u32[]{:S(2)}) copy-start(u32[32]{0:T(128)} %constant.28) | copy-start | bytes 388
  6.5 4.3 %copy-start.3 = (s32[128]{0:T(128)S(1)}, s32[128]{0:T(128)}, u32[]{:S(2)}) copy-start(s32[128]{0:T(128)} %param.6) | copy-start | bytes 1540
  6.5 4.3 %copy-start.2 = (f32[5]{0:T(128)S(1)}, f32[5]{0:T(128)}, u32[]{:S(2)}) copy-start(f32[5]{0:T(128)} %param.7) | copy-start | bytes 64
  6.5 40.4 %all-reduce.4.cloned.1.call-start = ((), (), s32[]{:S(2)}) async-start(), calls=%async_computation.2 | async-start | bytes 524288 | tf_op jit(solution)/shard_map/psum | solution.py:8
  10.8 62.2 %reduce-scatter.3.cloned.1.call-start = ((), (), s32[]{:S(2)}) async-start(), calls=%async_computation.3 | async-start | bytes 786432 | tf_op jit(solution)/shard_map/reduce_scatter | solution.py:65
  61.3 3.7 %copy-start.1 = (bf16[256,1024]{1,0:T(8,128)(2,1)}, bf16[256,1024]{1,0:T(8,128)(2,1)S(1)}, u32[]{:S(2)}) copy-start(bf16[256,1024]{1,0:T(8,128)(2,1)S(1)} %all_gather.14) | copy-start | bytes 1572868
  66.1 34.0 %reduce-scatter.5.cloned.1.call-start = ((), (), s32[]{:S(2)}) async-start(), calls=%async_computation.4 | async-start | bytes 327680 | tf_op jit(solution)/shard_map/reduce_scatter | solution.py:56
  68.2 69.9 %all-reduce.6.cloned.1.call-start = ((), (), s32[]{:S(2)}) async-start(), calls=%async_computation.5 | async-start | bytes 524288 | tf_op jit(solution)/shard_map/psum | solution.py:8
Sparse Core Ops, SparseCore 0:
  10.9 36.0 all-reduce.3
  66.3 6.6 reduce-scatter.2
  75.7 24.3 reduce-scatter.4
  103.6 34.4 all-reduce.5
where the time goes:
time: 150 us; the launch traced here: 147 us
  waiting for transfers between devices  82.7 us (55%)
  blocking collectives  26.2 us (17%)
  between operations  16.9 us (11%)
  matrix products  11.8 us (8%)
  other arithmetic  5.45 us (4%)
  local copies, waits for them, and re-layouts  4.31 us (3%)
    psum x2, waiting for transfers between devices, tensor_sum(): return lax.psum(value.astype(jnp.bfloat16), 'tensor').astype(jnp.float32)  52.6 us
    reduce_scatter x1, waiting for transfers between devices, shards(): lax.psum_scatter((lead[:, None] * own_rows.astype(jnp.float32) - other).a...  25.4 us
    unnamed x1, blocking collectives  8.7 us
    all_gather x1, blocking collectives, shards(): lax.all_gather(own_z, 'col', axis=0, tiled=True)  6.92 us
    all_gather x1, blocking collectives, shards(): lax.all_gather(proj_full, 'row', axis=0, tiled=True)  6.44 us
    reduce_scatter x1, waiting for transfers between devices, shards(): lax.psum_scatter((lead[:, None] * own_rows.astype(jnp.float32) - jnp.dot(...  4.65 us
    all_gather x1, blocking collectives, shards(): lax.all_gather(signs, 'row', axis=0, tiled=True)  4.16 us
    dot_general x1, matrix products, shards(): lax.dot_general(row_z, col_z, (((1,), (1,)), ((), ())), preferred_element...  3.53 us
  transfers between devices with their start and end apart: 4, of which 4 were waited for; matrix products, arithmetic and copies ran while one was open for 4% of the time, Pallas kernels for 0%

commit v1 on v0

v1 whole, which is shorter than its diff:
```python
import functools
import jax
import jax.numpy as jnp
from jax import lax
from jax.experimental import pallas as pl
from jax.experimental.pallas import tpu as pltpu
from jax.sharding import PartitionSpec as P

MESH = pl.DeviceIdType.MESH
PARTS = 2
NT_DIMS = (((1,), (1,)), ((), ()))


def kernel(
    n_tensor, n_row, n_col, n_rates,
    f_hbm, w_hbm, flags_ref, rates_ref, out_ref,
    f_ref, w_ref, part_ref, mine_ref, rs_ref, z_ref, s_ref, acc_ref, sum_ref,
    load_sem, rs_send, rs_recv, t_send, t_recv, c_send, c_recv, r_send, r_recv, s_send, s_recv,
):
    t, r, c = lax.axis_index("tensor"), lax.axis_index("row"), lax.axis_index("col")
    group = f_ref.shape[0]
    quarter = group // n_tensor
    depth, wide = w_ref.shape[1], w_ref.shape[2]
    width = wide * PARTS
    bits = [1 << b for b in range(n_col.bit_length() - 1)]

    def base(col, row):
        return pl.multiple_of((col * n_row + row) * group, group)

    def block(h, col, row, tpos):
        start = pl.multiple_of((col * n_row + row) * group + tpos * quarter, quarter)
        return z_ref.at[h, pl.ds(start, quarter), :]

    sends = []

    def push(src, dst, send, recv, **to):
        copy = pltpu.make_async_remote_copy(
            src_ref=src, dst_ref=dst, send_sem=send, recv_sem=recv, device_id=to, device_id_type=MESH
        )
        copy.start()
        sends.append(copy)

    def arrived(dst, recv):
        pltpu.make_async_copy(dst, dst, recv).wait()

    loads = [pltpu.make_async_copy(f_hbm, f_ref, load_sem.at[PARTS])]
    for h in range(PARTS):
        loads.append(
            pltpu.make_async_copy(w_hbm.at[:, pl.ds(h * wide, wide)], w_ref.at[h], load_sem.at[h])
        )
    for load in loads:
        load.start()

    barrier = pltpu.get_barrier_semaphore()
    near = [(dr, dc) for dr in range(n_row) for dc in range(n_col) if (dr, dc) != (0, 0)]
    for k in range(1, n_tensor):
        pl.semaphore_signal(
            barrier, inc=1, device_id={"tensor": lax.rem(t + k, n_tensor)}, device_id_type=MESH
        )
    for dr, dc in near:
        pl.semaphore_signal(
            barrier,
            inc=1,
            device_id={"row": lax.rem(r + dr, n_row), "col": lax.rem(c + dc, n_col)},
            device_id_type=MESH,
        )

    s_ref[c * n_row + r] = jnp.broadcast_to(
        (1 - 2 * flags_ref[...]).astype(jnp.float32), s_ref.shape[1:]
    )
    acc_ref[...] = jnp.zeros_like(acc_ref)
    sum_ref[...] = jnp.zeros_like(sum_ref)

    loads[0].wait()
    for h in range(PARTS):
        loads[1 + h].wait()
        partial = jnp.dot(f_ref[...], w_ref[h], preferred_element_type=jnp.float32)
        part_ref[h] = partial.astype(jnp.bfloat16)
        mine_ref[...] = partial
        if h == 0:
            pl.semaphore_wait(barrier, n_tensor - 1 + len(near))
        for k in range(1, n_tensor):
            peer = lax.rem(t + k, n_tensor)
            rows = pl.ds(pl.multiple_of(peer * quarter, quarter), quarter)
            push(
                part_ref.at[h, rows, :], rs_ref.at[h, k - 1],
                rs_send.at[h, k - 1], rs_recv.at[h, k - 1], tensor=peer,
            )
        own = mine_ref[pl.ds(pl.multiple_of(t * quarter, quarter), quarter), :]
        acc_ref[h, 0:quarter, :] = own
    for index, (dr, dc) in enumerate(near):
        push(
            s_ref.at[c * n_row + r], s_ref.at[c * n_row + r], s_send.at[index], s_recv.at[index],
            row=lax.rem(r + dr, n_row), col=lax.rem(c + dc, n_col),
        )

    order = [bits if h % 2 == 0 else bits[::-1] for h in range(PARTS)]

    def to_cols(h, k, mask, step):
        for j in range(step, len(bits)):
            tpos = lax.rem(t - k + n_tensor, n_tensor)
            src = block(h, jnp.bitwise_xor(c, mask), r, tpos)
            got = mask ^ order[h][j]
            push(
                src, src, c_send.at[h, k, got], c_recv.at[h, k, got],
                col=jnp.bitwise_xor(c, order[h][j]),
            )

    def to_rows(h, mask):
        src = z_ref.at[h, pl.ds(base(jnp.bitwise_xor(c, mask), r), group), :]
        for k in range(1, n_row):
            push(
                src, src, r_send.at[h, mask, k - 1], r_recv.at[h, mask, k - 1],
                row=lax.rem(r + k, n_row),
            )

    for h in range(PARTS):
        total = acc_ref[h, 0:quarter, :]
        for k in range(1, n_tensor):
            arrived(rs_ref.at[h, k - 1], rs_recv.at[h, k - 1])
            total = total + rs_ref[h, k - 1].astype(jnp.float32)
        start = pl.multiple_of((c * n_row + r) * group + t * quarter, quarter)
        z_ref[h, pl.ds(start, quarter), :] = total.astype(jnp.bfloat16)
        for k in range(1, n_tensor):
            src = block(h, c, r, t)
            push(
                src, src, t_send.at[h, k - 1], t_recv.at[h, k - 1], tensor=lax.rem(t + k, n_tensor)
            )
        to_cols(h, 0, 0, 0)
    for k in range(1, n_tensor):
        for h in range(PARTS):
            tpos = lax.rem(t - k + n_tensor, n_tensor)
            arrived(block(h, c, r, tpos), t_recv.at[h, k - 1])
            to_cols(h, k, 0, 0)
    for h in range(PARTS):
        to_rows(h, 0)

    acc_ref[...] = jnp.zeros_like(acc_ref)
    for index, (dr, dc) in enumerate(near):
        from_r, from_c = lax.rem(r - dr + n_row, n_row), lax.rem(c - dc + n_col, n_col)
        arrived(s_ref.at[from_c * n_row + from_r], s_recv.at[index])

    own_rows = pl.ds(base(c, r), group)
    own_norm = jnp.zeros((group, 1), jnp.float32)
    for h in range(PARTS):
        own_norm += jnp.sum(jnp.square(z_ref[h, own_rows, :].astype(jnp.float32)), axis=1, keepdims=True)

    def pairs(col, row, count):
        rows = pl.ds(base(col, row), count * group)
        cross = jnp.zeros((group, count * group), jnp.float32)
        norm = jnp.zeros((count * group, 1), jnp.float32)
        for h in range(PARTS):
            other = z_ref[h, rows, :]
            norm += jnp.sum(jnp.square(other.astype(jnp.float32)), axis=1, keepdims=True)
            cross += lax.dot_general(
                z_ref[h, own_rows, :], other, NT_DIMS, preferred_element_type=jnp.float32
            )
        norm = jnp.transpose(jnp.broadcast_to(norm, (count * group, 128)))[0:1, :]
        sign = jnp.concatenate([s_ref[col * n_row + row + i][0:1, :] for i in range(count)], axis=1)
        dist = jnp.maximum(own_norm + norm - 2.0 * cross, 0.0) * (1.0 / width)
        mixed = jnp.zeros_like(dist)
        for band in range(n_rates):
            mixed = mixed + rates_ref[band] * jnp.exp(-rates_ref[band] * dist)
        mixed = mixed * sign
        sum_ref[...] += jnp.sum(mixed, axis=1, keepdims=True)
        rounded = mixed.astype(jnp.bfloat16)
        for h in range(PARTS):
            acc_ref[h] += jnp.dot(rounded, z_ref[h, rows, :], preferred_element_type=jnp.float32)

    def column(mask):
        col = jnp.bitwise_xor(c, mask)
        for h in range(PARTS):
            for k in range(1, n_row):
                from_r = lax.rem(r - k + n_row, n_row)
                arrived(
                    z_ref.at[h, pl.ds(base(col, from_r), group), :], r_recv.at[h, mask, k - 1]
                )
        count = 2 if n_row % 2 == 0 else 1
        if n_row <= 2:
            pairs(col, 0, count)
        else:
            pl.loop(0, n_row // count)(lambda i: pairs(col, i * count, count))

    for step in range(len(bits)):
        masks = [[0] for _ in range(PARTS)]
        for h in range(PARTS):
            for j in range(step):
                masks[h] = masks[h] + [m ^ order[h][j] for m in masks[h]]
        for place in range(len(masks[0])):
            for k in range(n_tensor):
                for h in range(PARTS):
                    mask = masks[h][place] ^ order[h][step]
                    tpos = lax.rem(t - k + n_tensor, n_tensor)
                    arrived(block(h, jnp.bitwise_xor(c, mask), r, tpos), c_recv.at[h, k, mask])
                    to_cols(h, k, mask, step + 1)
            for h in range(PARTS):
                to_rows(h, masks[h][place] ^ order[h][step])
        if step == 0:
            column(0)
    for mask in range(1, n_col):
        column(mask)

    lead = jnp.transpose(jnp.broadcast_to(s_ref[c * n_row + r][0:1, :], (128, group)))[:, 0:1]
    lead = lead * (-32.0 / width)
    grads = []
    for h in range(PARTS):
        own = z_ref[h, own_rows, :].astype(jnp.float32)
        grads.append((lead * (sum_ref[...] * own - acc_ref[h])).astype(jnp.bfloat16))
    tile = 512
    for at in range(0, depth, tile):
        result = jnp.zeros((group, tile), jnp.float32)
        for h in range(PARTS):
            result += lax.dot_general(
                grads[h], w_ref[h, at : at + tile, :], NT_DIMS, preferred_element_type=jnp.float32
            )
        out_ref[:, at : at + tile] = result.astype(jnp.bfloat16)
    for copy in sends:
        copy.wait_send()


def shards(features, w_proj, flags, rates):
    n_tensor, n_row, n_col = (lax.axis_size(name) for name in ("tensor", "row", "col"))
    group, depth = features.shape
    width = w_proj.shape[1]
    wide = width // PARTS
    quarter = group // n_tensor
    rows = group * n_row * n_col
    near = n_row * n_col - 1
    dma = pltpu.SemaphoreType.DMA
    return pl.pallas_call(
        functools.partial(kernel, n_tensor, n_row, n_col, rates.shape[0]),
        out_shape=jax.ShapeDtypeStruct((group, depth), jnp.bfloat16),
        in_specs=[
            pl.BlockSpec(memory_space=pl.ANY),
            pl.BlockSpec(memory_space=pl.ANY),
            pl.BlockSpec(memory_space=pltpu.VMEM),
            pl.BlockSpec(memory_space=pltpu.SMEM),
        ],
        out_specs=pl.BlockSpec(memory_space=pltpu.VMEM),
        scratch_shapes=[
            pltpu.VMEM((group, depth), jnp.bfloat16),
            pltpu.VMEM((PARTS, depth, wide), jnp.bfloat16),
            pltpu.VMEM((PARTS, group, wide), jnp.bfloat16),
            pltpu.VMEM((group, wide), jnp.float32),
            pltpu.VMEM((PARTS, n_tensor - 1, quarter, wide), jnp.bfloat16),
            pltpu.VMEM((PARTS, rows, wide), jnp.bfloat16),
            pltpu.VMEM((n_row * n_col, 8, group), jnp.float32),
            pltpu.VMEM((PARTS, group, wide), jnp.float32),
            pltpu.VMEM((group, 1), jnp.float32),
            dma((PARTS + 1,)),
            dma((PARTS, n_tensor - 1)),
            dma((PARTS, n_tensor - 1)),
            dma((PARTS, n_tensor - 1)),
            dma((PARTS, n_tensor - 1)),
            dma((PARTS, n_tensor, n_col)),
            dma((PARTS, n_tensor, n_col)),
            dma((PARTS, n_col, n_row - 1)),
            dma((PARTS, n_col, n_row - 1)),
            dma((near,)),
            dma((near,)),
        ],
        compiler_params=pltpu.CompilerParams(
            collective_id=0, has_side_effects=True, vmem_limit_bytes=56 * 1024 * 1024
        ),
        cost_estimate=pl.CostEstimate(
            flops=4 * group * depth * width + 4 * group * rows * width,
            bytes_accessed=2 * (depth * width + 2 * group * depth),
            transcendentals=rates.shape[0] * group * rows,
        ),
        name="mmd",
    )(features, w_proj, flags.reshape(1, group), rates)


def solution(mesh):
    in_specs = (P(("row", "col"), "tensor"), P("tensor", None), P(("row", "col")), P())
    out_specs = P(("row", "col"), "tensor")
    return jax.shard_map(shards, mesh=mesh, in_specs=in_specs, out_specs=out_specs, check_vma=False)
```

time: 150 us -> 34.7 us (0.23); the launches traced: 147 us -> 34.3 us
  waiting for transfers between devices: 82.7 us -> 0 us
  Pallas kernels: 0 us -> 32.6 us
  blocking collectives: 26.2 us -> 0 us
  between operations: 16.9 us -> 0.01 us
  matrix products: 11.8 us -> 0 us
  other arithmetic: 5.45 us -> 0 us
  local copies, waits for them, and re-layouts: 4.31 us -> 1.77 us
    psum x2 -> x0, waiting for transfers between devices: 52.6 us -> none  [tensor_sum(): return lax.psum(value.astype(jnp.bfloat16), 'tensor').astype(jnp.float32)]
    pallas_call x0 -> x1, Pallas kernels: none -> 32.6 us  [shards(): pl.pallas_call(functools.partial(kernel, n_tensor, n_row, n_col, rates.sh...]
    reduce_scatter x2 -> x0, waiting for transfers between devices: 30.1 us -> none  [the longest x1 25.4 us: shards(): lax.psum_scatter((lead[:, None] * own_rows.astype(jnp.float32) - other).a...]
    all_gather x3 -> x0, blocking collectives: 17.5 us -> none  [the longest x1 6.92 us: shards(): lax.all_gather(own_z, 'col', axis=0, tiled=True)]
    dot_general x5 -> x0, matrix products: 11.8 us -> none  [the longest x1 3.53 us: shards(): lax.dot_general(row_z, col_z, (((1,), (1,)), ((), ())), preferred_element...]
    unnamed x1 -> x0, blocking collectives: 8.7 us -> none
    convert_element_type x3 -> x0, other arithmetic: 3.57 us -> none  [the longest x1 1.79 us: shards(): row_part = lax.psum_scatter((lead[:, None] * own_rows.astype(jnp.float32)...]
    add x1 -> x0, other arithmetic: 1.56 us -> none  [shards(): grad_z = tensor_sum(row_part + placed).astype(jnp.bfloat16)]
  transfers between devices with their start and end apart: 4 -> 0, of which waited for: 4 -> 0; matrix products, arithmetic and copies ran while one was open for 4% -> 0% of each run, Pallas kernels for 0% -> 0%
where the time goes in v1:
time: 34.7 us; the launch traced here: 34.3 us
  Pallas kernels  32.6 us (94%)
  local copies, waits for them, and re-layouts  1.77 us (5%)
    pallas_call x1, Pallas kernels, shards(): pl.pallas_call(functools.partial(kernel, n_tensor, n_row, n_col, rates.sh...  32.6 us
    unnamed x1, local copies, waits for them, and re-layouts  1.77 us

profile of v1, /device:TPU:1, one launch (start us, length us, event | category | flops | bytes accessed | tf_op | source)
XLA Modules:
  0.0 34.3 jit_solution(3172605005538801529)
XLA Ops:
  0.0 32.6 %mmd.1 = bf16[128,1536]{1,0:T(8,128)(2,1)} custom-call(bf16[128,1536]{1,0:T(8,128)(2,1)} %f_hbm.1, bf16[1536,1024]{1,0:T(8,128)(2,1)} %w_hbm.1, s32[1,128]{1,0:T(1,128)} %bitcast.1, f32[5]{0:T(128)} %rates_ref.1), custom_call_target="tpu_custom_call" | custom-call | flops 1342177280 | bytes 3932160 | tf_op jit(solution)/shard_map/mmd/pallas_call | solution.py:230
  32.6 1.8 %copy.6 = bf16[128,1536]{1,0:T(8,128)(2,1)} copy(bf16[128,1536]{1,0:T(8,128)(2,1)} %mmd.1) | data formatting | bytes 786432

commit v2 on v1

--- a/solution.py
+++ b/solution.py
@@ -7,14 +7,14 @@
 from jax.sharding import PartitionSpec as P
 
 MESH = pl.DeviceIdType.MESH
-PARTS = 2
+PARTS = 4
 NT_DIMS = (((1,), (1,)), ((), ()))
 
 
 def kernel(
     n_tensor, n_row, n_col, n_rates,
     f_hbm, w_hbm, flags_ref, rates_ref, out_ref,
-    f_ref, w_ref, part_ref, mine_ref, rs_ref, z_ref, s_ref, acc_ref, sum_ref,
+    f_ref, w_ref, part_ref, rs_ref, z_ref, s_ref, acc_ref, sum_ref,
     load_sem, rs_send, rs_recv, t_send, t_recv, c_send, c_recv, r_send, r_recv, s_send, s_recv,
 ):
     t, r, c = lax.axis_index("tensor"), lax.axis_index("row"), lax.axis_index("col")
@@ -68,15 +68,41 @@
     s_ref[c * n_row + r] = jnp.broadcast_to(
         (1 - 2 * flags_ref[...]).astype(jnp.float32), s_ref.shape[1:]
     )
-    acc_ref[...] = jnp.zeros_like(acc_ref)
-    sum_ref[...] = jnp.zeros_like(sum_ref)
-
-    loads[0].wait()
-    for h in range(PARTS):
+    order = [bits if h % 2 == 0 else bits[::-1] for h in range(PARTS)]
+    hops = []
+    for j in range(n_tensor - 1):
+        k = jnp.int32(0)
+        for at in range(n_tensor):
+            nearest = sorted((x for x in range(n_tensor) if x != at), key=lambda x: (abs(x - at), x))
+            k = k + jnp.where(t == at, (at - nearest[j]) % n_tensor, 0)
+        hops.append(k)
+    ks = [0] + hops
+
+    def of(k):
+        return lax.rem(t - k + n_tensor, n_tensor)
+
+    def to_cols(h, k, mask, step):
+        for j in range(step, len(bits)):
+            src = block(h, jnp.bitwise_xor(c, mask), r, of(k))
+            got = mask ^ order[h][j]
+            push(
+                src, src, c_send.at[h, k, got], c_recv.at[h, k, got],
+                col=jnp.bitwise_xor(c, order[h][j]),
+            )
+
+    def to_rows(h, mask):
+        src = z_ref.at[h, pl.ds(base(jnp.bitwise_xor(c, mask), r), group), :]
+        for k in range(1, n_row):
+            push(
+                src, src, r_send.at[h, mask, k - 1], r_recv.at[h, mask, k - 1],
+                row=lax.rem(r + k, n_row),
+            )
+
+    def project(h):
         loads[1 + h].wait()
         partial = jnp.dot(f_ref[...], w_ref[h], preferred_element_type=jnp.float32)
         part_ref[h] = partial.astype(jnp.bfloat16)
-        mine_ref[...] = partial
+        acc_ref[h] = partial
         if h == 0:
             pl.semaphore_wait(barrier, n_tensor - 1 + len(near))
         for k in range(1, n_tensor):
@@ -86,64 +112,76 @@
                 part_ref.at[h, rows, :], rs_ref.at[h, k - 1],
                 rs_send.at[h, k - 1], rs_recv.at[h, k - 1], tensor=peer,
             )
-        own = mine_ref[pl.ds(pl.multiple_of(t * quarter, quarter), quarter), :]
-        acc_ref[h, 0:quarter, :] = own
-    for index, (dr, dc) in enumerate(near):
-        push(
-            s_ref.at[c * n_row + r], s_ref.at[c * n_row + r], s_send.at[index], s_recv.at[index],
-            row=lax.rem(r + dr, n_row), col=lax.rem(c + dc, n_col),
-        )
-
-    order = [bits if h % 2 == 0 else bits[::-1] for h in range(PARTS)]
-
-    def to_cols(h, k, mask, step):
-        for j in range(step, len(bits)):
-            tpos = lax.rem(t - k + n_tensor, n_tensor)
-            src = block(h, jnp.bitwise_xor(c, mask), r, tpos)
-            got = mask ^ order[h][j]
-            push(
-                src, src, c_send.at[h, k, got], c_recv.at[h, k, got],
-                col=jnp.bitwise_xor(c, order[h][j]),
-            )
-
-    def to_rows(h, mask):
-        src = z_ref.at[h, pl.ds(base(jnp.bitwise_xor(c, mask), r), group), :]
-        for k in range(1, n_row):
-            push(
-                src, src, r_send.at[h, mask, k - 1], r_recv.at[h, mask, k - 1],
-                row=lax.rem(r + k, n_row),
-            )
-
-    for h in range(PARTS):
-        total = acc_ref[h, 0:quarter, :]
+
+    def line(h, k, right, left):
+        src = block(h, c, r, of(k))
+        for index, (cond, near_k, there) in enumerate(
+            ((right, lax.rem(k + 1, n_tensor), t + 1), (left, lax.rem(k - 1 + n_tensor, n_tensor), t - 1))
+        ):
+            slot = jnp.maximum(near_k - 1, 0)
+            copy = pltpu.make_async_remote_copy(
+                src_ref=src, dst_ref=src, send_sem=t_send.at[h, k, index], recv_sem=t_recv.at[h, slot],
+                device_id={"tensor": lax.rem(there + n_tensor, n_tensor)}, device_id_type=MESH,
+            )
+            pl.when(cond)(copy.start)
+            lines.append((cond, copy))
+
+    lines = []
+
+    def combine(h):
+        total = acc_ref[h, pl.ds(pl.multiple_of(t * quarter, quarter), quarter), :]
         for k in range(1, n_tensor):
             arrived(rs_ref.at[h, k - 1], rs_recv.at[h, k - 1])
             total = total + rs_ref[h, k - 1].astype(jnp.float32)
         start = pl.multiple_of((c * n_row + r) * group + t * quarter, quarter)
         z_ref[h, pl.ds(start, quarter), :] = total.astype(jnp.bfloat16)
-        for k in range(1, n_tensor):
-            src = block(h, c, r, t)
-            push(
-                src, src, t_send.at[h, k - 1], t_recv.at[h, k - 1], tensor=lax.rem(t + k, n_tensor)
-            )
+        line(h, 0, t < n_tensor - 1, t > 0)
         to_cols(h, 0, 0, 0)
-    for k in range(1, n_tensor):
-        for h in range(PARTS):
-            tpos = lax.rem(t - k + n_tensor, n_tensor)
-            arrived(block(h, c, r, tpos), t_recv.at[h, k - 1])
+
+    def gather_line(h):
+        for k in hops:
+            arrived(block(h, c, r, of(k)), t_recv.at[h, k - 1])
+            line(h, k, (t >= k) & (t < n_tensor - 1), (t < k) & (t > 0))
             to_cols(h, k, 0, 0)
-    for h in range(PARTS):
         to_rows(h, 0)
 
+    def gather_cols(h, step, mask):
+        for k in ks:
+            arrived(block(h, jnp.bitwise_xor(c, mask), r, of(k)), c_recv.at[h, k, mask])
+            to_cols(h, k, mask, step + 1)
+        to_rows(h, mask)
+
+    loads[0].wait()
+    for s in range(PARTS + 4):
+        if s < PARTS:
+            project(s)
+        if s == 0:
+            for index, (dr, dc) in enumerate(near):
+                push(
+                    s_ref.at[c * n_row + r], s_ref.at[c * n_row + r], s_send.at[index], s_recv.at[index],
+                    row=lax.rem(r + dr, n_row), col=lax.rem(c + dc, n_col),
+                )
+        if 0 <= s - 3 < PARTS:
+            gather_line(s - 3)
+        if 0 <= s - 1 < PARTS:
+            combine(s - 1)
+        if bits and 0 <= s - 4 < PARTS:
+            gather_cols(s - 4, 0, order[s - 4][0])
+
     acc_ref[...] = jnp.zeros_like(acc_ref)
+    sum_ref[...] = jnp.zeros_like(sum_ref)
     for index, (dr, dc) in enumerate(near):
         from_r, from_c = lax.rem(r - dr + n_row, n_row), lax.rem(c - dc + n_col, n_col)
         arrived(s_ref.at[from_c * n_row + from_r], s_recv.at[index])
 
+    def own_norms():
+        norm = jnp.zeros((group, 1), jnp.float32)
+        for h in range(PARTS):
+            norm += jnp.sum(jnp.square(z_ref[h, own_rows, :].astype(jnp.float32)), axis=1, keepdims=True)
+        return norm
+
     own_rows = pl.ds(base(c, r), group)
-    own_norm = jnp.zeros((group, 1), jnp.float32)
-    for h in range(PARTS):
-        own_norm += jnp.sum(jnp.square(z_ref[h, own_rows, :].astype(jnp.float32)), axis=1, keepdims=True)
+    own_norm = own_norms()
 
     def pairs(col, row, count):
         rows = pl.ds(base(col, row), count * group)
@@ -181,23 +219,33 @@
         else:
             pl.loop(0, n_row // count)(lambda i: pairs(col, i * count, count))
 
-    for step in range(len(bits)):
+    arrived_parts = {0: PARTS}
+    ready, finished = [0], []
+
+    def note(mask):
+        arrived_parts[mask] = arrived_parts.get(mask, 0) + 1
+        if arrived_parts[mask] == PARTS:
+            finished.append(mask)
+
+    for h in range(PARTS):
+        if bits:
+            note(order[h][0])
+    for step in range(1, len(bits)):
         masks = [[0] for _ in range(PARTS)]
         for h in range(PARTS):
             for j in range(step):
                 masks[h] = masks[h] + [m ^ order[h][j] for m in masks[h]]
         for place in range(len(masks[0])):
-            for k in range(n_tensor):
-                for h in range(PARTS):
-                    mask = masks[h][place] ^ order[h][step]
-                    tpos = lax.rem(t - k + n_tensor, n_tensor)
-                    arrived(block(h, jnp.bitwise_xor(c, mask), r, tpos), c_recv.at[h, k, mask])
-                    to_cols(h, k, mask, step + 1)
             for h in range(PARTS):
-                to_rows(h, masks[h][place] ^ order[h][step])
-        if step == 0:
-            column(0)
-    for mask in range(1, n_col):
+                mask = masks[h][place] ^ order[h][step]
+                gather_cols(h, step, mask)
+                note(mask)
+                if place > 0 and 0 < h < PARTS - 1 and ready:
+                    column(ready.pop(0))
+            if place == 0 and ready:
+                column(ready.pop(0))
+            ready, finished = ready + finished, []
+    for mask in ready + finished:
         column(mask)
 
     lead = jnp.transpose(jnp.broadcast_to(s_ref[c * n_row + r][0:1, :], (128, group)))[:, 0:1]
@@ -216,6 +264,8 @@
         out_ref[:, at : at + tile] = result.astype(jnp.bfloat16)
     for copy in sends:
         copy.wait_send()
+    for cond, copy in lines:
+        pl.when(cond)(copy.wait_send)
 
 
 def shards(features, w_proj, flags, rates):
@@ -231,8 +281,8 @@
         functools.partial(kernel, n_tensor, n_row, n_col, rates.shape[0]),
         out_shape=jax.ShapeDtypeStruct((group, depth), jnp.bfloat16),
         in_specs=[
-            pl.BlockSpec(memory_space=pl.ANY),
-            pl.BlockSpec(memory_space=pl.ANY),
+            pl.BlockSpec(memory_space=pltpu.HBM),
+            pl.BlockSpec(memory_space=pltpu.HBM),
             pl.BlockSpec(memory_space=pltpu.VMEM),
             pl.BlockSpec(memory_space=pltpu.SMEM),
         ],
@@ -241,7 +291,6 @@
             pltpu.VMEM((group, depth), jnp.bfloat16),
             pltpu.VMEM((PARTS, depth, wide), jnp.bfloat16),
             pltpu.VMEM((PARTS, group, wide), jnp.bfloat16),
-            pltpu.VMEM((group, wide), jnp.float32),
             pltpu.VMEM((PARTS, n_tensor - 1, quarter, wide), jnp.bfloat16),
             pltpu.VMEM((PARTS, rows, wide), jnp.bfloat16),
             pltpu.VMEM((n_row * n_col, 8, group), jnp.float32),
@@ -250,7 +299,7 @@
             dma((PARTS + 1,)),
             dma((PARTS, n_tensor - 1)),
             dma((PARTS, n_tensor - 1)),
-            dma((PARTS, n_tensor - 1)),
+            dma((PARTS, n_tensor, 2)),
             dma((PARTS, n_tensor - 1)),
             dma((PARTS, n_tensor, n_col)),
             dma((PARTS, n_tensor, n_col)),

time: 34.7 us -> 43.5 us (1.25)
  Pallas kernels: 32.6 us -> 41.5 us
    pallas_call x1, Pallas kernels: 32.6 us -> 41.5 us  [shards(): pl.pallas_call(functools.partial(kernel, n_tensor, n_row, n_col, rates.sh...]
where the time goes in v2:
time: 43.5 us; the launch traced here: 43.3 us
  Pallas kernels  41.5 us (95%)
  local copies, waits for them, and re-layouts  1.77 us (4%)
    pallas_call x1, Pallas kernels, shards(): pl.pallas_call(functools.partial(kernel, n_tensor, n_row, n_col, rates.sh...  41.5 us
    unnamed x1, local copies, waits for them, and re-layouts  1.77 us

profile of v2, /device:TPU:1, one launch (start us, length us, event | category | flops | bytes accessed | tf_op | source)
XLA Modules:
  0.0 43.3 jit_solution(13917036780122062118)
XLA Ops:
  0.0 41.5 %mmd.1 = bf16[128,1536]{1,0:T(8,128)(2,1)} custom-call(bf16[128,1536]{1,0:T(8,128)(2,1)} %f_hbm.1, bf16[1536,1024]{1,0:T(8,128)(2,1)} %w_hbm.1, s32[1,128]{1,0:T(1,128)} %bitcast.1, f32[5]{0:T(128)} %rates_ref.1), custom_call_target="tpu_custom_call" | custom-call | flops 1342177280 | bytes 3932160 | tf_op jit(solution)/shard_map/mmd/pallas_call | solution.py:280
  41.6 1.8 %copy.6 = bf16[128,1536]{1,0:T(8,128)(2,1)} copy(bf16[128,1536]{1,0:T(8,128)(2,1)} %mmd.1) | data formatting | bytes 786432

commit v3 on v1

v3 whole, which is shorter than its diff:
```python
import functools
import jax
import jax.numpy as jnp
from jax import lax
from jax.experimental import pallas as pl
from jax.experimental.pallas import tpu as pltpu
from jax.sharding import PartitionSpec as P

MESH = pl.DeviceIdType.MESH
PARTS = 2
NT_DIMS = (((1,), (1,)), ((), ()))


def kernel(
    n_tensor, n_row, n_col, n_rates,
    f_ref, w_hbm, flags_ref, rates_ref, out_ref,
    w_ref, part_ref, rs_ref, z_ref, s_ref, acc_ref, sum_ref,
    load_sem, rs_send, rs_recv, t_send, t_recv, c_send, c_recv, r_send, r_recv, s_send, s_recv,
):
    t, r, c = lax.axis_index("tensor"), lax.axis_index("row"), lax.axis_index("col")
    group = f_ref.shape[0]
    quarter = group // n_tensor
    depth, wide = w_ref.shape[1], w_ref.shape[2]
    width = wide * PARTS
    bits = [1 << b for b in range(n_col.bit_length() - 1)]
    order = [bits if h % 2 == 0 else bits[::-1] for h in range(PARTS)]
    runs = [(0, 1), (1, n_tensor)] if n_tensor > 1 else [(0, 1)]

    def slot(h, mask, dr, first=0, last=n_tensor):
        start = (mask * n_row + dr) * group
        return z_ref.at[h, start + first * quarter : start + last * quarter, :]

    sends = []

    def push(src, dst, send, recv, **to):
        copy = pltpu.make_async_remote_copy(
            src_ref=src, dst_ref=dst, send_sem=send, recv_sem=recv, device_id=to, device_id_type=MESH
        )
        copy.start()
        sends.append(copy)

    def arrived(dst, recv):
        pltpu.make_async_copy(dst, dst, recv).wait()

    loads = [
        pltpu.make_async_copy(w_hbm.at[:, h * wide : (h + 1) * wide], w_ref.at[h], load_sem.at[h])
        for h in range(PARTS)
    ]
    loads[0].start()

    barrier = pltpu.get_barrier_semaphore()
    near = [(dr, dc) for dr in range(n_row) for dc in range(n_col) if (dr, dc) != (0, 0)]
    for k in range(1, n_tensor):
        pl.semaphore_signal(
            barrier, inc=1, device_id={"tensor": lax.rem(t + k, n_tensor)}, device_id_type=MESH
        )
    for dr, mask in near:
        pl.semaphore_signal(
            barrier,
            inc=1,
            device_id={"row": lax.rem(r + dr, n_row), "col": jnp.bitwise_xor(c, mask)},
            device_id_type=MESH,
        )

    came = lax.broadcasted_iota(jnp.int32, (group, group), 0)
    goes = lax.broadcasted_iota(jnp.int32, (group, group), 1)
    goes = goes + t * quarter
    turn = (came == jnp.where(goes >= group, goes - group, goes)).astype(jnp.bfloat16)
    signs = jnp.broadcast_to((1 - 2 * flags_ref[...]).astype(jnp.float32), s_ref.shape[1:])
    s_ref[0] = jnp.dot(signs.astype(jnp.bfloat16), turn, preferred_element_type=jnp.float32)

    for h in range(PARTS):
        loads[h].wait()
        if h + 1 < PARTS:
            loads[h + 1].start()
        partial = jnp.dot(f_ref[...], w_ref[h], preferred_element_type=jnp.float32)
        part_ref[h] = partial.astype(jnp.bfloat16)
        acc_ref[h] = partial
        if h == 0:
            pl.semaphore_wait(barrier, n_tensor - 1 + len(near))
        for k in range(1, n_tensor):
            peer = lax.rem(t + k, n_tensor)
            rows = pl.ds(pl.multiple_of(peer * quarter, quarter), quarter)
            push(
                part_ref.at[h, rows, :], rs_ref.at[h, k - 1],
                rs_send.at[h, k - 1], rs_recv.at[h, k - 1], tensor=peer,
            )
    for index, (dr, mask) in enumerate(near):
        push(
            s_ref.at[0], s_ref.at[mask * n_row + dr], s_send.at[index], s_recv.at[index],
            row=lax.rem(r + dr, n_row), col=jnp.bitwise_xor(c, mask),
        )

    def to_cols(h, run, mask, step):
        for bit in order[h][step:]:
            push(
                slot(h, mask, 0, *runs[run]), slot(h, mask ^ bit, 0, *runs[run]),
                c_send.at[h, run, mask ^ bit], c_recv.at[h, run, mask ^ bit],
                col=jnp.bitwise_xor(c, bit),
            )

    def to_rows(h, mask):
        for dr in range(1, n_row):
            push(
                slot(h, mask, 0), slot(h, mask, dr),
                r_send.at[h, mask, dr - 1], r_recv.at[h, mask, dr - 1], row=lax.rem(r + dr, n_row),
            )

    def gather_cols(h, step, mask):
        for run in range(len(runs)):
            arrived(slot(h, mask, 0, *runs[run]), c_recv.at[h, run, mask])
            to_cols(h, run, mask, step + 1)
        to_rows(h, mask)

    for h in range(PARTS):
        total = acc_ref[h, pl.ds(pl.multiple_of(t * quarter, quarter), quarter), :]
        for k in range(1, n_tensor):
            arrived(rs_ref.at[h, k - 1], rs_recv.at[h, k - 1])
            total = total + rs_ref[h, k - 1].astype(jnp.float32)
        z_ref[h, 0:quarter, :] = total.astype(jnp.bfloat16)
        for k in range(1, n_tensor):
            push(
                slot(h, 0, 0, 0, 1), slot(h, 0, 0, k, k + 1), t_send.at[h, k - 1], t_recv.at[h, k - 1],
                tensor=lax.rem(t + n_tensor - k, n_tensor),
            )
        to_cols(h, 0, 0, 0)
    for h in range(PARTS):
        for k in range(1, n_tensor):
            arrived(slot(h, 0, 0, k, k + 1), t_recv.at[h, k - 1])
        if n_tensor > 1:
            to_cols(h, 1, 0, 0)
        to_rows(h, 0)

    acc_ref[...] = jnp.zeros_like(acc_ref)
    sum_ref[...] = jnp.zeros_like(sum_ref)
    for index, (dr, mask) in enumerate(near):
        arrived(s_ref.at[mask * n_row + dr], s_recv.at[index])

    own_norm = jnp.zeros((group, 1), jnp.float32)
    for h in range(PARTS):
        own_norm += jnp.sum(
            jnp.square(z_ref[h, 0:group, :].astype(jnp.float32)), axis=1, keepdims=True
        )

    def pairs(first, count):
        if isinstance(first, int):
            rows = slice(first * group, (first + count) * group)
        else:
            rows = pl.ds(pl.multiple_of(first * group, group), count * group)
        cross = jnp.zeros((group, count * group), jnp.float32)
        norm = jnp.zeros((count * group, 1), jnp.float32)
        for h in range(PARTS):
            other = z_ref[h, rows, :]
            norm += jnp.sum(jnp.square(other.astype(jnp.float32)), axis=1, keepdims=True)
            cross += lax.dot_general(
                z_ref[h, 0:group, :], other, NT_DIMS, preferred_element_type=jnp.float32
            )
        norm = jnp.transpose(jnp.broadcast_to(norm, (count * group, 128)))[0:1, :]
        sign = jnp.concatenate([s_ref[first + i][0:1, :] for i in range(count)], axis=1)
        dist = jnp.maximum(own_norm + norm - 2.0 * cross, 0.0) * (1.0 / width)
        mixed = jnp.zeros_like(dist)
        for band in range(n_rates):
            mixed = mixed + rates_ref[band] * jnp.exp(-rates_ref[band] * dist)
        mixed = mixed * sign
        sum_ref[...] += jnp.sum(mixed, axis=1, keepdims=True)
        rounded = mixed.astype(jnp.bfloat16)
        for h in range(PARTS):
            acc_ref[h] += jnp.dot(rounded, z_ref[h, rows, :], preferred_element_type=jnp.float32)

    def column(mask):
        for h in range(PARTS):
            for dr in range(1, n_row):
                arrived(slot(h, mask, dr), r_recv.at[h, mask, dr - 1])
        count = 2 if n_row % 2 == 0 else 1
        if n_row <= 2:
            pairs(mask * n_row, count)
        else:
            pl.loop(0, n_row // count)(lambda i: pairs(mask * n_row + i * count, count))

    have = {0: PARTS}
    ready, finished = [0], []
    for step in range(len(bits)):
        masks = [[0] for _ in range(PARTS)]
        for h in range(PARTS):
            for j in range(step):
                masks[h] = masks[h] + [m ^ order[h][j] for m in masks[h]]
        for place in range(len(masks[0])):
            for h in range(PARTS):
                mask = masks[h][place] ^ order[h][step]
                gather_cols(h, step, mask)
                have[mask] = have.get(mask, 0) + 1
                if have[mask] == PARTS:
                    finished.append(mask)
                if place > 0 and ready:
                    column(ready.pop(0))
            if step > 0 and place == 0 and ready:
                column(ready.pop(0))
            ready, finished = ready + finished, []
    for mask in ready + finished:
        column(mask)

    lead = jnp.transpose(jnp.broadcast_to(s_ref[0][0:1, :], (128, group)))[:, 0:1]
    lead = lead * (-32.0 / width)
    grads = []
    for h in range(PARTS):
        own = z_ref[h, 0:group, :].astype(jnp.float32)
        grads.append((lead * (sum_ref[...] * own - acc_ref[h])).astype(jnp.bfloat16))
    tile = 512
    for at in range(0, depth, tile):
        result = jnp.zeros((group, tile), jnp.float32)
        for h in range(PARTS):
            result += lax.dot_general(
                grads[h], w_ref[h, at : at + tile, :], NT_DIMS, preferred_element_type=jnp.float32
            )
        result = result.astype(jnp.bfloat16)
        for k in range(n_tensor):
            rows = pl.ds(pl.multiple_of(lax.rem(t + k, n_tensor) * quarter, quarter), quarter)
            out_ref[rows, at : at + tile] = result[k * quarter : (k + 1) * quarter]
    for copy in sends:
        copy.wait_send()


def shards(features, w_proj, flags, rates):
    n_tensor, n_row, n_col = (lax.axis_size(name) for name in ("tensor", "row", "col"))
    group, depth = features.shape
    width = w_proj.shape[1]
    wide = width // PARTS
    quarter = group // n_tensor
    rows = group * n_row * n_col
    near = n_row * n_col - 1
    dma = pltpu.SemaphoreType.DMA
    return pl.pallas_call(
        functools.partial(kernel, n_tensor, n_row, n_col, rates.shape[0]),
        out_shape=jax.ShapeDtypeStruct((group, depth), jnp.bfloat16),
        in_specs=[
            pl.BlockSpec(memory_space=pltpu.VMEM),
            pl.BlockSpec(memory_space=pltpu.HBM),
            pl.BlockSpec(memory_space=pltpu.VMEM),
            pl.BlockSpec(memory_space=pltpu.SMEM),
        ],
        out_specs=pl.BlockSpec(memory_space=pltpu.VMEM),
        scratch_shapes=[
            pltpu.VMEM((PARTS, depth, wide), jnp.bfloat16),
            pltpu.VMEM((PARTS, group, wide), jnp.bfloat16),
            pltpu.VMEM((PARTS, n_tensor - 1, quarter, wide), jnp.bfloat16),
            pltpu.VMEM((PARTS, rows, wide), jnp.bfloat16),
            pltpu.VMEM((n_row * n_col, 8, group), jnp.float32),
            pltpu.VMEM((PARTS, group, wide), jnp.float32),
            pltpu.VMEM((group, 1), jnp.float32),
            dma((PARTS,)),
            dma((PARTS, n_tensor - 1)),
            dma((PARTS, n_tensor - 1)),
            dma((PARTS, n_tensor - 1)),
            dma((PARTS, n_tensor - 1)),
            dma((PARTS, 2, n_col)),
            dma((PARTS, 2, n_col)),
            dma((PARTS, n_col, n_row - 1)),
            dma((PARTS, n_col, n_row - 1)),
            dma((near,)),
            dma((near,)),
        ],
        compiler_params=pltpu.CompilerParams(
            collective_id=0, has_side_effects=True, vmem_limit_bytes=52 * 1024 * 1024
        ),
        cost_estimate=pl.CostEstimate(
            flops=4 * group * depth * width + 4 * group * rows * width,
            bytes_accessed=2 * (depth * width + 2 * group * depth),
            transcendentals=rates.shape[0] * group * rows,
        ),
        name="mmd",
    )(features, w_proj, flags.reshape(1, group), rates)


def solution(mesh):
    in_specs = (P(("row", "col"), "tensor"), P("tensor", None), P(("row", "col")), P())
    out_specs = P(("row", "col"), "tensor")
    return jax.shard_map(shards, mesh=mesh, in_specs=in_specs, out_specs=out_specs, check_vma=False)
```

time: 34.7 us -> 35.4 us (1.020)
  local copies, waits for them, and re-layouts: 1.77 us -> 3.05 us
  Pallas kernels: 32.6 us -> 32.1 us
    unnamed x1 -> x7, local copies, waits for them, and re-layouts: 1.77 us -> 3.05 us
    pallas_call x1, Pallas kernels: 32.6 us -> 32.1 us  [shards(): pl.pallas_call(functools.partial(kernel, n_tensor, n_row, n_col, rates.sh...]
where the time goes in v3:
time: 35.4 us; the launch traced here: 35.2 us
  Pallas kernels  32.1 us (91%)
  local copies, waits for them, and re-layouts  3.05 us (9%)
    pallas_call x1, Pallas kernels, shards(): pl.pallas_call(functools.partial(kernel, n_tensor, n_row, n_col, rates.sh...  32.1 us
    unnamed x7, local copies, waits for them, and re-layouts  3.05 us

profile of v3, /device:TPU:1, one launch (start us, length us, event | category | flops | bytes accessed | tf_op | source)
XLA Modules:
  0.0 35.2 jit_solution(5797033233400071052)
XLA Ops:
  0.0 0.0 copy-start
  0.0 1.0 %copy-done = bf16[128,1536]{1,0:T(8,128)(2,1)S(1)} copy-done((bf16[128,1536]{1,0:T(8,128)(2,1)S(1)}, bf16[128,1536]{1,0:T(8,128)(2,1)}, u32[]{:S(2)}) %copy-start) | copy-done | bytes 393240
  1.0 0.0 copy-start.1
  1.0 0.7 %copy-done.1 = s32[128]{0:T(128)S(1)} copy-done((s32[128]{0:T(128)S(1)}, s32[128]{0:T(128)}, u32[]{:S(2)}) %copy-start.1) | copy-done | bytes 536
  1.7 0.0 copy-start.2
  1.7 0.7 %copy-done.2 = f32[5]{0:T(128)S(1)} copy-done((f32[5]{0:T(128)S(1)}, f32[5]{0:T(128)}, u32[]{:S(2)}) %copy-start.2) | copy-done | bytes 44
  2.3 32.1 %mmd.1 = bf16[128,1536]{1,0:T(8,128)(2,1)S(1)} custom-call(bf16[128,1536]{1,0:T(8,128)(2,1)S(1)} %copy-done, bf16[1536,1024]{1,0:T(8,128)(2,1)} %w_hbm.1, s32[1,128]{1,0:T(1,128)S(1)} %bitcast.1, f32[5]{0:T(128)S(1)} %copy-done.2), custom_call_target="tpu_custom_call" | custom-call | flops 1342177280 | bytes 3932160 | tf_op jit(solution)/shard_map/mmd/pallas_call | solution.py:232
  34.4 0.7 %copy.6 = bf16[128,1536]{1,0:T(8,128)(2,1)} copy(bf16[128,1536]{1,0:T(8,128)(2,1)S(1)} %mmd.1) | data formatting | bytes 786432
Async XLA Ops:
  0.0 1.0 %copy-start = (bf16[128,1536]{1,0:T(8,128)(2,1)S(1)}, bf16[128,1536]{1,0:T(8,128)(2,1)}, u32[]{:S(2)}) copy-start(bf16[128,1536]{1,0:T(8,128)(2,1)} %f_ref.1) | copy-start | bytes 1179652
  1.0 0.7 %copy-start.1 = (s32[128]{0:T(128)S(1)}, s32[128]{0:T(128)}, u32[]{:S(2)}) copy-start(s32[128]{0:T(128)} %param.6) | copy-start | bytes 1540
  1.7 0.7 %copy-start.2 = (f32[5]{0:T(128)S(1)}, f32[5]{0:T(128)}, u32[]{:S(2)}) copy-start(f32[5]{0:T(128)} %rates_ref.1) | copy-start | bytes 64

commit v4 on v3

--- a/solution.py
+++ b/solution.py
@@ -13,8 +13,8 @@
 
 def kernel(
     n_tensor, n_row, n_col, n_rates,
-    f_ref, w_hbm, flags_ref, rates_ref, out_ref,
-    w_ref, part_ref, rs_ref, z_ref, s_ref, acc_ref, sum_ref,
+    f_hbm, w_hbm, flags_ref, rates_ref, out_ref,
+    f_ref, w_ref, part_ref, own_ref, rs_ref, z_ref, s_ref, acc_ref, sum_ref,
     load_sem, rs_send, rs_recv, t_send, t_recv, c_send, c_recv, r_send, r_recv, s_send, s_recv,
 ):
     t, r, c = lax.axis_index("tensor"), lax.axis_index("row"), lax.axis_index("col")
@@ -46,6 +46,8 @@
         pltpu.make_async_copy(w_hbm.at[:, h * wide : (h + 1) * wide], w_ref.at[h], load_sem.at[h])
         for h in range(PARTS)
     ]
+    loads.append(pltpu.make_async_copy(f_hbm, f_ref, load_sem.at[PARTS]))
+    loads[PARTS].start()
     loads[0].start()
 
     barrier = pltpu.get_barrier_semaphore()
@@ -69,22 +71,50 @@
     signs = jnp.broadcast_to((1 - 2 * flags_ref[...]).astype(jnp.float32), s_ref.shape[1:])
     s_ref[0] = jnp.dot(signs.astype(jnp.bfloat16), turn, preferred_element_type=jnp.float32)
 
+    places = [0]
+    halvings = n_tensor.bit_length() - 1
+    for step in range(halvings):
+        places = [2 * p for p in places] + [2 * p + 1 for p in places]
+
+    def quarters(first, last):
+        return slice(first * quarter, last * quarter)
+
+    def halve(h, step):
+        count = n_tensor >> (step + 1)
+        push(
+            part_ref.at[h, quarters(count, 2 * count), :], rs_ref.at[h, quarters(count, 2 * count), :],
+            rs_send.at[h, step], rs_recv.at[h, step], tensor=jnp.bitwise_xor(t, 1 << step),
+        )
+
+    def halved(h, step):
+        count = n_tensor >> (step + 1)
+        landed = rs_ref.at[h, quarters(count, 2 * count), :]
+        arrived(landed, rs_recv.at[h, step])
+        total = acc_ref[h, quarters(0, count), :] + landed[...].astype(jnp.float32)
+        if count == 1:
+            z_ref[h, 0:quarter, :] = total.astype(jnp.bfloat16)
+        else:
+            half = count // 2 * quarter
+            acc_ref[h, 0:half, :] = total[:half]
+            part_ref[h, half : 2 * half, :] = total[half:].astype(jnp.bfloat16)
+            halve(h, step + 1)
+
+    loads[PARTS].wait()
     for h in range(PARTS):
         loads[h].wait()
         if h + 1 < PARTS:
             loads[h + 1].start()
-        partial = jnp.dot(f_ref[...], w_ref[h], preferred_element_type=jnp.float32)
-        part_ref[h] = partial.astype(jnp.bfloat16)
-        acc_ref[h] = partial
+        own_ref[...] = jnp.dot(f_ref[...], w_ref[h], preferred_element_type=jnp.float32)
+        for index, place in enumerate(places):
+            start = pl.multiple_of(jnp.bitwise_xor(t, place) * quarter, quarter)
+            rows = own_ref[pl.ds(start, quarter), :]
+            if 2 * index < n_tensor:
+                acc_ref[h, quarters(index, index + 1), :] = rows
+            else:
+                part_ref[h, quarters(index, index + 1), :] = rows.astype(jnp.bfloat16)
         if h == 0:
             pl.semaphore_wait(barrier, n_tensor - 1 + len(near))
-        for k in range(1, n_tensor):
-            peer = lax.rem(t + k, n_tensor)
-            rows = pl.ds(pl.multiple_of(peer * quarter, quarter), quarter)
-            push(
-                part_ref.at[h, rows, :], rs_ref.at[h, k - 1],
-                rs_send.at[h, k - 1], rs_recv.at[h, k - 1], tensor=peer,
-            )
+        halve(h, 0)
     for index, (dr, mask) in enumerate(near):
         push(
             s_ref.at[0], s_ref.at[mask * n_row + dr], s_send.at[index], s_recv.at[index],
@@ -112,12 +142,11 @@
             to_cols(h, run, mask, step + 1)
         to_rows(h, mask)
 
-    for h in range(PARTS):
-        total = acc_ref[h, pl.ds(pl.multiple_of(t * quarter, quarter), quarter), :]
-        for k in range(1, n_tensor):
-            arrived(rs_ref.at[h, k - 1], rs_recv.at[h, k - 1])
-            total = total + rs_ref[h, k - 1].astype(jnp.float32)
-        z_ref[h, 0:quarter, :] = total.astype(jnp.bfloat16)
+    for step in range(halvings - 1):
+        for h in range(PARTS):
+            halved(h, step)
+    for h in range(PARTS):
+        halved(h, halvings - 1)
         for k in range(1, n_tensor):
             push(
                 slot(h, 0, 0, 0, 1), slot(h, 0, 0, k, k + 1), t_send.at[h, k - 1], t_recv.at[h, k - 1],
@@ -205,17 +234,10 @@
     for h in range(PARTS):
         own = z_ref[h, 0:group, :].astype(jnp.float32)
         grads.append((lead * (sum_ref[...] * own - acc_ref[h])).astype(jnp.bfloat16))
-    tile = 512
-    for at in range(0, depth, tile):
-        result = jnp.zeros((group, tile), jnp.float32)
-        for h in range(PARTS):
-            result += lax.dot_general(
-                grads[h], w_ref[h, at : at + tile, :], NT_DIMS, preferred_element_type=jnp.float32
-            )
-        result = result.astype(jnp.bfloat16)
+    for h in range(PARTS):
         for k in range(n_tensor):
             rows = pl.ds(pl.multiple_of(lax.rem(t + k, n_tensor) * quarter, quarter), quarter)
-            out_ref[rows, at : at + tile] = result[k * quarter : (k + 1) * quarter]
+            out_ref[rows, h * wide : (h + 1) * wide] = grads[h][k * quarter : (k + 1) * quarter]
     for copy in sends:
         copy.wait_send()
 
@@ -229,25 +251,27 @@
     rows = group * n_row * n_col
     near = n_row * n_col - 1
     dma = pltpu.SemaphoreType.DMA
-    return pl.pallas_call(
+    grad_z = pl.pallas_call(
         functools.partial(kernel, n_tensor, n_row, n_col, rates.shape[0]),
-        out_shape=jax.ShapeDtypeStruct((group, depth), jnp.bfloat16),
+        out_shape=jax.ShapeDtypeStruct((group, width), jnp.bfloat16),
         in_specs=[
-            pl.BlockSpec(memory_space=pltpu.VMEM),
+            pl.BlockSpec(memory_space=pltpu.HBM),
             pl.BlockSpec(memory_space=pltpu.HBM),
             pl.BlockSpec(memory_space=pltpu.VMEM),
             pl.BlockSpec(memory_space=pltpu.SMEM),
         ],
         out_specs=pl.BlockSpec(memory_space=pltpu.VMEM),
         scratch_shapes=[
+            pltpu.VMEM((group, depth), jnp.bfloat16),
             pltpu.VMEM((PARTS, depth, wide), jnp.bfloat16),
             pltpu.VMEM((PARTS, group, wide), jnp.bfloat16),
-            pltpu.VMEM((PARTS, n_tensor - 1, quarter, wide), jnp.bfloat16),
+            pltpu.VMEM((group, wide), jnp.float32),
+            pltpu.VMEM((PARTS, group, wide), jnp.bfloat16),
             pltpu.VMEM((PARTS, rows, wide), jnp.bfloat16),
             pltpu.VMEM((n_row * n_col, 8, group), jnp.float32),
             pltpu.VMEM((PARTS, group, wide), jnp.float32),
             pltpu.VMEM((group, 1), jnp.float32),
-            dma((PARTS,)),
+            dma((PARTS + 1,)),
             dma((PARTS, n_tensor - 1)),
             dma((PARTS, n_tensor - 1)),
             dma((PARTS, n_tensor - 1)),
@@ -260,15 +284,17 @@
             dma((near,)),
         ],
         compiler_params=pltpu.CompilerParams(
-            collective_id=0, has_side_effects=True, vmem_limit_bytes=52 * 1024 * 1024
+            collective_id=0, has_side_effects=True, vmem_limit_bytes=56 * 1024 * 1024
         ),
         cost_estimate=pl.CostEstimate(
-            flops=4 * group * depth * width + 4 * group * rows * width,
+            flops=2 * group * depth * width + 4 * group * rows * width,
             bytes_accessed=2 * (depth * width + 2 * group * depth),
             transcendentals=rates.shape[0] * group * rows,
         ),
         name="mmd",
     )(features, w_proj, flags.reshape(1, group), rates)
+    result = lax.dot_general(grad_z, w_proj, NT_DIMS, preferred_element_type=jnp.float32)
+    return result.astype(jnp.bfloat16)
 
 
 def solution(mesh):

time: 35.4 us -> 36 us (1.017)
  local copies, waits for them, and re-layouts: 3.05 us -> 0.01 us
  matrix products: 0 us -> 2.87 us
  Pallas kernels: 32.1 us -> 32.9 us
    unnamed x7 -> x2, local copies, waits for them, and re-layouts: 3.05 us -> 0.01 us
    dot_general x0 -> x1, matrix products: none -> 2.87 us  [shards(): lax.dot_general(grad_z, w_proj, NT_DIMS, preferred_element_type=jnp.float32)]
    pallas_call x1, Pallas kernels: 32.1 us -> 32.9 us  [shards(): pl.pallas_call(functools.partial(kernel, n_tensor, n_row, n_col, rates.sh...]
where the time goes in v4:
time: 36 us; the launch traced here: 35.8 us
  Pallas kernels  32.9 us (91%)
  matrix products  2.87 us (8%)
    pallas_call x1, Pallas kernels, shards(): pl.pallas_call(functools.partial(kernel, n_tensor, n_row, n_col, rates.sh...  32.9 us
    dot_general x1, matrix products, shards(): lax.dot_general(grad_z, w_proj, NT_DIMS, preferred_element_type=jnp.float32)  2.87 us

profile of v4, /device:TPU:1, one launch (start us, length us, event | category | flops | bytes accessed | tf_op | source)
XLA Modules:
  0.0 35.8 jit_solution(5978752231664436491)
XLA Ops:
  0.0 0.0 copy-start
  0.0 32.9 %mmd.1 = bf16[128,1024]{1,0:T(8,128)(2,1)} custom-call(bf16[128,1536]{1,0:T(8,128)(2,1)} %f_hbm.1, bf16[1536,1024]{1,0:T(8,128)(2,1)} %w_hbm.1, s32[1,128]{1,0:T(1,128)} %bitcast.3, f32[5]{0:T(128)} %rates_ref.1), custom_call_target="tpu_custom_call" | custom-call | flops 939524096 | bytes 3932160 | tf_op jit(solution)/shard_map/mmd/pallas_call | solution.py:254
  32.9 0.0 copy-done
  33.0 2.9 %convolution_convert_fusion = bf16[128,1536]{1,0:T(8,128)(2,1)} fusion(bf16[128,1024]{1,0:T(8,128)(2,1)} %mmd.1, bf16[1536,1024]{1,0:T(8,128)(2,1)S(1)} %copy-done), kind=kOutput, calls=%fused_computation | convolution fusion | flops 402849792 | bytes 3801088 | tf_op jit(solution)/shard_map/dot_general | solution.py:296
Async XLA Ops:
  0.0 32.9 %copy-start = (bf16[1536,1024]{1,0:T(8,128)(2,1)S(1)}, bf16[1536,1024]{1,0:T(8,128)(2,1)}, u32[]{:S(2)}) copy-start(bf16[1536,1024]{1,0:T(8,128)(2,1)} %w_hbm.1) | copy-start | bytes 9437188

commit v5 on v4

--- a/solution.py
+++ b/solution.py
@@ -7,7 +7,7 @@
 from jax.sharding import PartitionSpec as P
 
 MESH = pl.DeviceIdType.MESH
-PARTS = 2
+PARTS = 4
 NT_DIMS = (((1,), (1,)), ((), ()))
 
 
@@ -142,17 +142,21 @@
             to_cols(h, run, mask, step + 1)
         to_rows(h, mask)
 
-    for step in range(halvings - 1):
-        for h in range(PARTS):
-            halved(h, step)
-    for h in range(PARTS):
-        halved(h, halvings - 1)
+    def spread(h):
         for k in range(1, n_tensor):
             push(
                 slot(h, 0, 0, 0, 1), slot(h, 0, 0, k, k + 1), t_send.at[h, k - 1], t_recv.at[h, k - 1],
                 tensor=lax.rem(t + n_tensor - k, n_tensor),
             )
         to_cols(h, 0, 0, 0)
+
+    for turn_at in range(PARTS + halvings - 1):
+        for h in range(PARTS):
+            step = turn_at - h
+            if 0 <= step < halvings:
+                halved(h, step)
+                if step == halvings - 1:
+                    spread(h)
     for h in range(PARTS):
         for k in range(1, n_tensor):
             arrived(slot(h, 0, 0, k, k + 1), t_recv.at[h, k - 1])

time: 36 us -> 42.3 us (1.17)
  Pallas kernels: 32.9 us -> 39.2 us
    pallas_call x1, Pallas kernels: 32.9 us -> 39.2 us  [shards(): pl.pallas_call(functools.partial(kernel, n_tensor, n_row, n_col, rates.sh...]
where the time goes in v5:
time: 42.3 us; the launch traced here: 42.1 us
  Pallas kernels  39.2 us (93%)
  matrix products  2.87 us (7%)
    pallas_call x1, Pallas kernels, shards(): pl.pallas_call(functools.partial(kernel, n_tensor, n_row, n_col, rates.sh...  39.2 us
    dot_general x1, matrix products, shards(): lax.dot_general(grad_z, w_proj, NT_DIMS, preferred_element_type=jnp.float32)  2.87 us

profile of v5, /device:TPU:1, one launch (start us, length us, event | category | flops | bytes accessed | tf_op | source)
XLA Modules:
  0.0 42.1 jit_solution(16366936871302650399)
XLA Ops:
  0.0 0.0 copy-start
  0.0 39.2 %mmd.1 = bf16[128,1024]{1,0:T(8,128)(2,1)} custom-call(bf16[128,1536]{1,0:T(8,128)(2,1)} %f_hbm.1, bf16[1536,1024]{1,0:T(8,128)(2,1)} %w_hbm.1, s32[1,128]{1,0:T(1,128)} %bitcast.3, f32[5]{0:T(128)} %rates_ref.1), custom_call_target="tpu_custom_call" | custom-call | flops 939524096 | bytes 3932160 | tf_op jit(solution)/shard_map/mmd/pallas_call | solution.py:258
  39.2 0.0 copy-done
  39.2 2.9 %convolution_convert_fusion = bf16[128,1536]{1,0:T(8,128)(2,1)} fusion(bf16[128,1024]{1,0:T(8,128)(2,1)} %mmd.1, bf16[1536,1024]{1,0:T(8,128)(2,1)S(1)} %copy-done), kind=kOutput, calls=%fused_computation | convolution fusion | flops 402849792 | bytes 3801088 | tf_op jit(solution)/shard_map/dot_general | solution.py:300
Async XLA Ops:
  0.0 39.2 %copy-start = (bf16[1536,1024]{1,0:T(8,128)(2,1)S(1)}, bf16[1536,1024]{1,0:T(8,128)(2,1)}, u32[]{:S(2)}) copy-start(bf16[1536,1024]{1,0:T(8,128)(2,1)} %w_hbm.1) | copy-start | bytes 9437188

commit v6 on v3

v6 whole, which is shorter than its diff:
```python
import functools
import jax
import jax.numpy as jnp
from jax import lax
from jax.experimental import pallas as pl
from jax.experimental.pallas import tpu as pltpu
from jax.sharding import PartitionSpec as P

MESH = pl.DeviceIdType.MESH
PARTS = 2
NT_DIMS = (((1,), (1,)), ((), ()))


def kernel(
    n_tensor, n_row, n_col, n_rates,
    f_hbm, w_hbm, flags_ref, rates_ref, out_ref,
    f_ref, w_ref, part_ref, own_ref, rs_ref, z_ref, s_ref, acc_ref, sum_ref,
    load_sem, rs_send, rs_recv, t_send, t_recv, c_send, c_recv, r_send, r_recv, s_send, s_recv,
):
    t, r, c = lax.axis_index("tensor"), lax.axis_index("row"), lax.axis_index("col")
    group = f_ref.shape[0]
    quarter = group // n_tensor
    wide = w_ref.shape[2]
    width = wide * PARTS
    bits = [1 << b for b in range(n_col.bit_length() - 1)]
    runs = [(0, n_tensor // 2), (n_tensor // 2, n_tensor)]
    order = [bits, bits[::-1]]

    def blocks(mask, first, last):
        return z_ref.at[mask * group + first * quarter : mask * group + last * quarter, :]

    def layer(dr, first, last):
        return z_ref.at[(dr * n_col + first) * group : (dr * n_col + last) * group, :]

    sends = []

    def push(src, dst, send, recv, **to):
        copy = pltpu.make_async_remote_copy(
            src_ref=src, dst_ref=dst, send_sem=send, recv_sem=recv, device_id=to, device_id_type=MESH
        )
        copy.start()
        sends.append(copy)

    def arrived(dst, recv):
        pltpu.make_async_copy(dst, dst, recv).wait()

    loads = [
        pltpu.make_async_copy(w_hbm.at[:, h * wide : (h + 1) * wide], w_ref.at[h], load_sem.at[h])
        for h in range(PARTS)
    ]
    loads.append(pltpu.make_async_copy(f_hbm, f_ref, load_sem.at[PARTS]))
    loads[PARTS].start()
    loads[0].start()

    barrier = pltpu.get_barrier_semaphore()
    peers = [{"tensor": lax.rem(t + k, n_tensor)} for k in range(1, n_tensor)]
    peers += [{"row": lax.rem(r + dr, n_row)} for dr in range(1, n_row)]
    peers += [{"col": jnp.bitwise_xor(c, bit)} for bit in bits]
    for peer in peers:
        pl.semaphore_signal(barrier, inc=1, device_id=peer, device_id_type=MESH)

    came = lax.broadcasted_iota(jnp.int32, (group, group), 0)
    goes = lax.broadcasted_iota(jnp.int32, (group, group), 1)
    goes = goes + t * quarter
    turn = (came == jnp.where(goes >= group, goes - group, goes)).astype(jnp.bfloat16)
    signs = jnp.broadcast_to((1 - 2 * flags_ref[...]).astype(jnp.float32), s_ref.shape[1:])
    s_ref[0] = jnp.dot(signs.astype(jnp.bfloat16), turn, preferred_element_type=jnp.float32)

    loads[PARTS].wait()
    for h in range(PARTS):
        loads[h].wait()
        if h + 1 < PARTS:
            loads[h + 1].start()
        partial = jnp.dot(f_ref[...], w_ref[h], preferred_element_type=jnp.float32)
        part_ref[h] = partial.astype(jnp.bfloat16)
        own_ref[h] = partial
        if h == 0:
            pl.semaphore_wait(barrier, len(peers))
        for k in range(1, n_tensor):
            peer = lax.rem(t + k, n_tensor)
            rows = pl.ds(pl.multiple_of(peer * quarter, quarter), quarter)
            push(
                part_ref.at[h, rows, :], rs_ref.at[h, k - 1],
                rs_send.at[h, k - 1], rs_recv.at[h, k - 1], tensor=peer,
            )

    for index, bit in enumerate(bits):
        push(
            s_ref.at[0:bit], s_ref.at[bit : 2 * bit], s_send.at[index], s_recv.at[index],
            col=jnp.bitwise_xor(c, bit),
        )
        arrived(s_ref.at[bit : 2 * bit], s_recv.at[index])
    for dr in range(1, n_row):
        index = len(bits) + dr - 1
        push(
            s_ref.at[0:n_col], s_ref.at[dr * n_col : (dr + 1) * n_col], s_send.at[index], s_recv.at[index],
            row=lax.rem(r + dr, n_row),
        )
    acc_ref[...] = jnp.zeros_like(acc_ref)
    sum_ref[...] = jnp.zeros_like(sum_ref)

    for h in range(PARTS):
        total = own_ref[h, pl.ds(pl.multiple_of(t * quarter, quarter), quarter), :]
        for k in range(1, n_tensor):
            arrived(rs_ref.at[h, k - 1], rs_recv.at[h, k - 1])
            total = total + rs_ref[h, k - 1].astype(jnp.float32)
        z_ref[0:quarter, h * wide : (h + 1) * wide] = total.astype(jnp.bfloat16)
    for k in range(1, n_tensor):
        push(
            blocks(0, 0, 1), blocks(0, k, k + 1), t_send.at[k - 1], t_recv.at[k - 1],
            tensor=lax.rem(t + n_tensor - k, n_tensor),
        )

    def to_cols(run, mask, step):
        for bit in order[run][step:]:
            push(
                blocks(mask, *runs[run]), blocks(mask ^ bit, *runs[run]),
                c_send.at[run, mask ^ bit], c_recv.at[run, mask ^ bit], col=jnp.bitwise_xor(c, bit),
            )

    for run, (first, last) in enumerate(runs):
        for k in range(max(first, 1), last):
            arrived(blocks(0, k, k + 1), t_recv.at[k - 1])
        to_cols(run, 0, 0)

    own_norm = jnp.sum(jnp.square(z_ref[0:group, :].astype(jnp.float32)), axis=1, keepdims=True)

    def pairs(first, count):
        if isinstance(first, int):
            rows = slice(first * group, (first + count) * group)
        else:
            rows = pl.ds(pl.multiple_of(first * group, group), count * group)
        other = z_ref[rows, :]
        norm = jnp.sum(jnp.square(other.astype(jnp.float32)), axis=1, keepdims=True)
        cross = lax.dot_general(
            z_ref[0:group, :], other, NT_DIMS, preferred_element_type=jnp.float32
        )
        norm = jnp.transpose(jnp.broadcast_to(norm, (count * group, 128)))[0:1, :]
        sign = jnp.concatenate([s_ref[first + i][0:1, :] for i in range(count)], axis=1)
        dist = jnp.maximum(own_norm + norm - 2.0 * cross, 0.0) * (1.0 / width)
        mixed = jnp.zeros_like(dist)
        for band in range(n_rates):
            mixed = mixed + rates_ref[band] * jnp.exp(-rates_ref[band] * dist)
        mixed = mixed * sign
        sum_ref[...] += jnp.sum(mixed, axis=1, keepdims=True)
        acc_ref[...] += jnp.dot(
            mixed.astype(jnp.bfloat16), z_ref[rows, :], preferred_element_type=jnp.float32
        )

    def most(dr):
        count = (n_col - 2) // 2
        if count > 1:
            pl.loop(0, count)(lambda i: pairs(dr * n_col + 2 * i, 2))
        else:
            pairs(dr * n_col, 2)

    def to_rows(part, first, last):
        for dr in range(1, n_row):
            push(
                layer(0, first, last), layer(dr, first, last),
                r_send.at[part, dr - 1], r_recv.at[part, dr - 1], row=lax.rem(r + dr, n_row),
            )

    for step in range(len(bits)):
        masks = [[0], [0]]
        for run in range(2):
            for j in range(step):
                masks[run] = masks[run] + [m ^ order[run][j] for m in masks[run]]
        for place in range(len(masks[0])):
            if step == len(bits) - 1 and place == len(masks[0]) - 1:
                to_rows(0, 0, n_col - 1)
                for index in range(len(bits), len(bits) + n_row - 1):
                    dr = index - len(bits) + 1
                    arrived(s_ref.at[dr * n_col : (dr + 1) * n_col], s_recv.at[index])
                most(0)
                for dr in range(1, n_row):
                    arrived(layer(dr, 0, n_col - 1), r_recv.at[0, dr - 1])
                    most(dr)
            for run in range(2):
                mask = masks[run][place] ^ order[run][step]
                arrived(blocks(mask, *runs[run]), c_recv.at[run, mask])
                to_cols(run, mask, step + 1)
    to_rows(1, n_col - 1, n_col)
    pairs(n_col - 2, 2)
    for dr in range(1, n_row):
        arrived(layer(dr, n_col - 1, n_col), r_recv.at[1, dr - 1])
        pairs(dr * n_col + n_col - 2, 2)

    lead = jnp.transpose(jnp.broadcast_to(s_ref[0][0:1, :], (128, group)))[:, 0:1]
    lead = lead * (-32.0 / width)
    own = z_ref[0:group, :].astype(jnp.float32)
    grads = (lead * (sum_ref[...] * own - acc_ref[...])).astype(jnp.bfloat16)
    for k in range(n_tensor):
        rows = pl.ds(pl.multiple_of(lax.rem(t + k, n_tensor) * quarter, quarter), quarter)
        out_ref[rows, :] = grads[k * quarter : (k + 1) * quarter]
    for copy in sends:
        copy.wait_send()


def shards(features, w_proj, flags, rates):
    n_tensor, n_row, n_col = (lax.axis_size(name) for name in ("tensor", "row", "col"))
    group, depth = features.shape
    width = w_proj.shape[1]
    wide = width // PARTS
    quarter = group // n_tensor
    rows = group * n_row * n_col
    hops = n_col.bit_length() - 1 + n_row - 1
    dma = pltpu.SemaphoreType.DMA
    grad_z = pl.pallas_call(
        functools.partial(kernel, n_tensor, n_row, n_col, rates.shape[0]),
        out_shape=jax.ShapeDtypeStruct((group, width), jnp.bfloat16),
        in_specs=[
            pl.BlockSpec(memory_space=pltpu.HBM),
            pl.BlockSpec(memory_space=pltpu.HBM),
            pl.BlockSpec(memory_space=pltpu.VMEM),
            pl.BlockSpec(memory_space=pltpu.SMEM),
        ],
        out_specs=pl.BlockSpec(memory_space=pltpu.VMEM),
        scratch_shapes=[
            pltpu.VMEM((group, depth), jnp.bfloat16),
            pltpu.VMEM((PARTS, depth, wide), jnp.bfloat16),
            pltpu.VMEM((PARTS, group, wide), jnp.bfloat16),
            pltpu.VMEM((PARTS, group, wide), jnp.float32),
            pltpu.VMEM((PARTS, n_tensor - 1, quarter, wide), jnp.bfloat16),
            pltpu.VMEM((rows, width), jnp.bfloat16),
            pltpu.VMEM((n_row * n_col, 8, group), jnp.float32),
            pltpu.VMEM((group, width), jnp.float32),
            pltpu.VMEM((group, 1), jnp.float32),
            dma((PARTS + 1,)),
            dma((PARTS, n_tensor - 1)),
            dma((PARTS, n_tensor - 1)),
            dma((n_tensor - 1,)),
            dma((n_tensor - 1,)),
            dma((2, n_col)),
            dma((2, n_col)),
            dma((2, n_row - 1)),
            dma((2, n_row - 1)),
            dma((hops,)),
            dma((hops,)),
        ],
        compiler_params=pltpu.CompilerParams(
            collective_id=0, has_side_effects=True, vmem_limit_bytes=56 * 1024 * 1024
        ),
        cost_estimate=pl.CostEstimate(
            flops=2 * group * depth * width + 4 * group * rows * width,
            bytes_accessed=2 * (depth * width + 2 * group * depth),
            transcendentals=rates.shape[0] * group * rows,
        ),
        name="mmd",
    )(features, w_proj, flags.reshape(1, group), rates)
    result = lax.dot_general(grad_z, w_proj, NT_DIMS, preferred_element_type=jnp.float32)
    return result.astype(jnp.bfloat16)


def solution(mesh):
    in_specs = (P(("row", "col"), "tensor"), P("tensor", None), P(("row", "col")), P())
    out_specs = P(("row", "col"), "tensor")
    return jax.shard_map(shards, mesh=mesh, in_specs=in_specs, out_specs=out_specs, check_vma=False)
```

time: 35.4 us -> 35.6 us (level)
  local copies, waits for them, and re-layouts: 3.05 us -> 0.01 us
  matrix products: 0 us -> 2.87 us
  Pallas kernels: 32.1 us -> 32.6 us
    unnamed x7 -> x2, local copies, waits for them, and re-layouts: 3.05 us -> 0.01 us
    dot_general x0 -> x1, matrix products: none -> 2.87 us  [shards(): lax.dot_general(grad_z, w_proj, NT_DIMS, preferred_element_type=jnp.float32)]
    pallas_call x1, Pallas kernels: 32.1 us -> 32.6 us  [shards(): pl.pallas_call(functools.partial(kernel, n_tensor, n_row, n_col, rates.sh...]
where the time goes in v6:
time: 35.6 us; the launch traced here: 35.5 us
  Pallas kernels  32.6 us (92%)
  matrix products  2.87 us (8%)
    pallas_call x1, Pallas kernels, shards(): pl.pallas_call(functools.partial(kernel, n_tensor, n_row, n_col, rates.sh...  32.6 us
    dot_general x1, matrix products, shards(): lax.dot_general(grad_z, w_proj, NT_DIMS, preferred_element_type=jnp.float32)  2.87 us

profile of v6, /device:TPU:1, one launch (start us, length us, event | category | flops | bytes accessed | tf_op | source)
XLA Modules:
  0.0 35.5 jit_solution(2494412004841642624)
XLA Ops:
  0.0 0.0 copy-start
  0.0 32.6 %mmd.1 = bf16[128,1024]{1,0:T(8,128)(2,1)} custom-call(bf16[128,1536]{1,0:T(8,128)(2,1)} %f_hbm.1, bf16[1536,1024]{1,0:T(8,128)(2,1)} %w_hbm.1, s32[1,128]{1,0:T(1,128)} %bitcast.3, f32[5]{0:T(128)} %rates_ref.1), custom_call_target="tpu_custom_call" | custom-call | flops 939524096 | bytes 3932160 | tf_op jit(solution)/shard_map/mmd/pallas_call | solution.py:209
  32.6 0.0 copy-done
  32.6 2.9 %convolution_convert_fusion = bf16[128,1536]{1,0:T(8,128)(2,1)} fusion(bf16[128,1024]{1,0:T(8,128)(2,1)} %mmd.1, bf16[1536,1024]{1,0:T(8,128)(2,1)S(1)} %copy-done), kind=kOutput, calls=%fused_computation | convolution fusion | flops 402849792 | bytes 3801088 | tf_op jit(solution)/shard_map/dot_general | solution.py:251
Async XLA Ops:
  0.0 32.6 %copy-start = (bf16[1536,1024]{1,0:T(8,128)(2,1)S(1)}, bf16[1536,1024]{1,0:T(8,128)(2,1)}, u32[]{:S(2)}) copy-start(bf16[1536,1024]{1,0:T(8,128)(2,1)} %w_hbm.1) | copy-start | bytes 9437188

commit v7 on v3

--- a/solution.py
+++ b/solution.py
@@ -13,8 +13,8 @@
 
 def kernel(
     n_tensor, n_row, n_col, n_rates,
-    f_ref, w_hbm, flags_ref, rates_ref, out_ref,
-    w_ref, part_ref, rs_ref, z_ref, s_ref, acc_ref, sum_ref,
+    f_hbm, w_hbm, flags_ref, rates_ref, out_ref,
+    f_ref, w_ref, part_ref, rs_ref, z_ref, s_ref, acc_ref, sum_ref,
     load_sem, rs_send, rs_recv, t_send, t_recv, c_send, c_recv, r_send, r_recv, s_send, s_recv,
 ):
     t, r, c = lax.axis_index("tensor"), lax.axis_index("row"), lax.axis_index("col")
@@ -46,21 +46,16 @@
         pltpu.make_async_copy(w_hbm.at[:, h * wide : (h + 1) * wide], w_ref.at[h], load_sem.at[h])
         for h in range(PARTS)
     ]
+    loads.append(pltpu.make_async_copy(f_hbm, f_ref, load_sem.at[PARTS]))
+    loads[PARTS].start()
     loads[0].start()
 
     barrier = pltpu.get_barrier_semaphore()
-    near = [(dr, dc) for dr in range(n_row) for dc in range(n_col) if (dr, dc) != (0, 0)]
-    for k in range(1, n_tensor):
-        pl.semaphore_signal(
-            barrier, inc=1, device_id={"tensor": lax.rem(t + k, n_tensor)}, device_id_type=MESH
-        )
-    for dr, mask in near:
-        pl.semaphore_signal(
-            barrier,
-            inc=1,
-            device_id={"row": lax.rem(r + dr, n_row), "col": jnp.bitwise_xor(c, mask)},
-            device_id_type=MESH,
-        )
+    peers = [{"tensor": lax.rem(t + k, n_tensor)} for k in range(1, n_tensor)]
+    peers += [{"row": lax.rem(r + dr, n_row)} for dr in range(1, n_row)]
+    peers += [{"col": jnp.bitwise_xor(c, bit)} for bit in bits]
+    for peer in peers:
+        pl.semaphore_signal(barrier, inc=1, device_id=peer, device_id_type=MESH)
 
     came = lax.broadcasted_iota(jnp.int32, (group, group), 0)
     goes = lax.broadcasted_iota(jnp.int32, (group, group), 1)
@@ -69,6 +64,7 @@
     signs = jnp.broadcast_to((1 - 2 * flags_ref[...]).astype(jnp.float32), s_ref.shape[1:])
     s_ref[0] = jnp.dot(signs.astype(jnp.bfloat16), turn, preferred_element_type=jnp.float32)
 
+    loads[PARTS].wait()
     for h in range(PARTS):
         loads[h].wait()
         if h + 1 < PARTS:
@@ -77,7 +73,7 @@
         part_ref[h] = partial.astype(jnp.bfloat16)
         acc_ref[h] = partial
         if h == 0:
-            pl.semaphore_wait(barrier, n_tensor - 1 + len(near))
+            pl.semaphore_wait(barrier, len(peers))
         for k in range(1, n_tensor):
             peer = lax.rem(t + k, n_tensor)
             rows = pl.ds(pl.multiple_of(peer * quarter, quarter), quarter)
@@ -85,11 +81,16 @@
                 part_ref.at[h, rows, :], rs_ref.at[h, k - 1],
                 rs_send.at[h, k - 1], rs_recv.at[h, k - 1], tensor=peer,
             )
-    for index, (dr, mask) in enumerate(near):
-        push(
-            s_ref.at[0], s_ref.at[mask * n_row + dr], s_send.at[index], s_recv.at[index],
-            row=lax.rem(r + dr, n_row), col=jnp.bitwise_xor(c, mask),
-        )
+    hops = [({"row": lax.rem(r + dr, n_row)}, 0, dr, 1) for dr in range(1, n_row)]
+    hops += [({"col": jnp.bitwise_xor(c, bit)}, 0, bit * n_row, bit * n_row) for bit in bits]
+    for index, (to, src, dst, count) in enumerate(hops):
+        landed = s_ref.at[dst : dst + count]
+        push(s_ref.at[src : src + count], landed, s_send.at[index], s_recv.at[index], **to)
+        if index >= n_row - 2 and index + 1 < len(hops):
+            for before in range(index + 1 if index == n_row - 2 else 0):
+                arrived(s_ref.at[hops[before][2] : hops[before][2] + 1], s_recv.at[before])
+            if index > n_row - 2:
+                arrived(landed, s_recv.at[index])
 
     def to_cols(h, run, mask, step):
         for bit in order[h][step:]:
@@ -133,8 +134,8 @@
 
     acc_ref[...] = jnp.zeros_like(acc_ref)
     sum_ref[...] = jnp.zeros_like(sum_ref)
-    for index, (dr, mask) in enumerate(near):
-        arrived(s_ref.at[mask * n_row + dr], s_recv.at[index])
+    last = hops[-1]
+    arrived(s_ref.at[last[2] : last[2] + last[3]], s_recv.at[len(hops) - 1])
 
     own_norm = jnp.zeros((group, 1), jnp.float32)
     for h in range(PARTS):
@@ -197,6 +198,9 @@
                 column(ready.pop(0))
             ready, finished = ready + finished, []
     for mask in ready + finished:
+        if mask == n_col - 1:
+            for copy in sends:
+                copy.wait_send()
         column(mask)
 
     lead = jnp.transpose(jnp.broadcast_to(s_ref[0][0:1, :], (128, group)))[:, 0:1]
@@ -205,19 +209,10 @@
     for h in range(PARTS):
         own = z_ref[h, 0:group, :].astype(jnp.float32)
         grads.append((lead * (sum_ref[...] * own - acc_ref[h])).astype(jnp.bfloat16))
-    tile = 512
-    for at in range(0, depth, tile):
-        result = jnp.zeros((group, tile), jnp.float32)
-        for h in range(PARTS):
-            result += lax.dot_general(
-                grads[h], w_ref[h, at : at + tile, :], NT_DIMS, preferred_element_type=jnp.float32
-            )
-        result = result.astype(jnp.bfloat16)
+    for h in range(PARTS):
         for k in range(n_tensor):
             rows = pl.ds(pl.multiple_of(lax.rem(t + k, n_tensor) * quarter, quarter), quarter)
-            out_ref[rows, at : at + tile] = result[k * quarter : (k + 1) * quarter]
-    for copy in sends:
-        copy.wait_send()
+            out_ref[rows, h * wide : (h + 1) * wide] = grads[h][k * quarter : (k + 1) * quarter]
 
 
 def shards(features, w_proj, flags, rates):
@@ -227,19 +222,20 @@
     wide = width // PARTS
     quarter = group // n_tensor
     rows = group * n_row * n_col
-    near = n_row * n_col - 1
+    near = n_row - 1 + n_col.bit_length() - 1
     dma = pltpu.SemaphoreType.DMA
-    return pl.pallas_call(
+    grad_z = pl.pallas_call(
         functools.partial(kernel, n_tensor, n_row, n_col, rates.shape[0]),
-        out_shape=jax.ShapeDtypeStruct((group, depth), jnp.bfloat16),
+        out_shape=jax.ShapeDtypeStruct((group, width), jnp.bfloat16),
         in_specs=[
-            pl.BlockSpec(memory_space=pltpu.VMEM),
+            pl.BlockSpec(memory_space=pltpu.HBM),
             pl.BlockSpec(memory_space=pltpu.HBM),
             pl.BlockSpec(memory_space=pltpu.VMEM),
             pl.BlockSpec(memory_space=pltpu.SMEM),
         ],
         out_specs=pl.BlockSpec(memory_space=pltpu.VMEM),
         scratch_shapes=[
+            pltpu.VMEM((group, depth), jnp.bfloat16),
             pltpu.VMEM((PARTS, depth, wide), jnp.bfloat16),
             pltpu.VMEM((PARTS, group, wide), jnp.bfloat16),
             pltpu.VMEM((PARTS, n_tensor - 1, quarter, wide), jnp.bfloat16),
@@ -247,7 +243,7 @@
             pltpu.VMEM((n_row * n_col, 8, group), jnp.float32),
             pltpu.VMEM((PARTS, group, wide), jnp.float32),
             pltpu.VMEM((group, 1), jnp.float32),
-            dma((PARTS,)),
+            dma((PARTS + 1,)),
             dma((PARTS, n_tensor - 1)),
             dma((PARTS, n_tensor - 1)),
             dma((PARTS, n_tensor - 1)),
@@ -260,15 +256,17 @@
             dma((near,)),
         ],
         compiler_params=pltpu.CompilerParams(
-            collective_id=0, has_side_effects=True, vmem_limit_bytes=52 * 1024 * 1024
+            collective_id=0, has_side_effects=True, vmem_limit_bytes=56 * 1024 * 1024
         ),
         cost_estimate=pl.CostEstimate(
-            flops=4 * group * depth * width + 4 * group * rows * width,
+            flops=2 * group * depth * width + 4 * group * rows * width,
             bytes_accessed=2 * (depth * width + 2 * group * depth),
             transcendentals=rates.shape[0] * group * rows,
         ),
         name="mmd",
     )(features, w_proj, flags.reshape(1, group), rates)
+    result = lax.dot_general(grad_z, w_proj, NT_DIMS, preferred_element_type=jnp.float32)
+    return result.astype(jnp.bfloat16)
 
 
 def solution(mesh):

time: 35.4 us -> 35.2 us (level)
  local copies, waits for them, and re-layouts: 3.05 us -> 0.01 us
  matrix products: 0 us -> 2.87 us
    unnamed x7 -> x2, local copies, waits for them, and re-layouts: 3.05 us -> 0.01 us
    dot_general x0 -> x1, matrix products: none -> 2.87 us  [shards(): lax.dot_general(grad_z, w_proj, NT_DIMS, preferred_element_type=jnp.float32)]
where the time goes in v7:
time: 35.2 us; the launch traced here: 34.9 us
  Pallas kernels  32 us (91%)
  matrix products  2.87 us (8%)
    pallas_call x1, Pallas kernels, shards(): pl.pallas_call(functools.partial(kernel, n_tensor, n_row, n_col, rates.sh...  32 us
    dot_general x1, matrix products, shards(): lax.dot_general(grad_z, w_proj, NT_DIMS, preferred_element_type=jnp.float32)  2.87 us

profile of v7, /device:TPU:1, one launch (start us, length us, event | category | flops | bytes accessed | tf_op | source)
XLA Modules:
  0.0 34.9 jit_solution(12778356370063679940)
XLA Ops:
  0.0 0.0 copy-start
  0.0 32.0 %mmd.1 = bf16[128,1024]{1,0:T(8,128)(2,1)} custom-call(bf16[128,1536]{1,0:T(8,128)(2,1)} %f_hbm.1, bf16[1536,1024]{1,0:T(8,128)(2,1)} %w_hbm.1, s32[1,128]{1,0:T(1,128)} %bitcast.3, f32[5]{0:T(128)} %rates_ref.1), custom_call_target="tpu_custom_call" | custom-call | flops 939524096 | bytes 3932160 | tf_op jit(solution)/shard_map/mmd/pallas_call | solution.py:227
  32.0 0.0 copy-done
  32.1 2.9 %convolution_convert_fusion = bf16[128,1536]{1,0:T(8,128)(2,1)} fusion(bf16[128,1024]{1,0:T(8,128)(2,1)} %mmd.1, bf16[1536,1024]{1,0:T(8,128)(2,1)S(1)} %copy-done), kind=kOutput, calls=%fused_computation | convolution fusion | flops 402849792 | bytes 3801088 | tf_op jit(solution)/shard_map/dot_general | solution.py:268
Async XLA Ops:
  0.0 32.0 %copy-start = (bf16[1536,1024]{1,0:T(8,128)(2,1)S(1)}, bf16[1536,1024]{1,0:T(8,128)(2,1)}, u32[]{:S(2)}) copy-start(bf16[1536,1024]{1,0:T(8,128)(2,1)} %w_hbm.1) | copy-start | bytes 9437188

commit v8 on v7

--- a/solution.py
+++ b/solution.py
@@ -213,6 +213,14 @@
         for k in range(n_tensor):
             rows = pl.ds(pl.multiple_of(lax.rem(t + k, n_tensor) * quarter, quarter), quarter)
             out_ref[rows, h * wide : (h + 1) * wide] = grads[h][k * quarter : (k + 1) * quarter]
+
+
+def product(grad_ref, w_ref, out_ref):
+    tile = 512
+    for at in range(0, out_ref.shape[1], tile):
+        out_ref[:, at : at + tile] = lax.dot_general(
+            grad_ref[...], w_ref[at : at + tile, :], NT_DIMS, preferred_element_type=jnp.float32
+        ).astype(jnp.bfloat16)
 
 
 def shards(features, w_proj, flags, rates):
@@ -265,8 +273,19 @@
         ),
         name="mmd",
     )(features, w_proj, flags.reshape(1, group), rates)
-    result = lax.dot_general(grad_z, w_proj, NT_DIMS, preferred_element_type=jnp.float32)
-    return result.astype(jnp.bfloat16)
+    return pl.pallas_call(
+        product,
+        out_shape=jax.ShapeDtypeStruct((group, depth), jnp.bfloat16),
+        in_specs=[pl.BlockSpec(memory_space=pltpu.VMEM)] * 2,
+        out_specs=pl.BlockSpec(memory_space=pltpu.VMEM),
+        compiler_params=pltpu.CompilerParams(vmem_limit_bytes=16 * 1024 * 1024),
+        cost_estimate=pl.CostEstimate(
+            flops=2 * group * depth * width,
+            bytes_accessed=2 * (depth * width + group * (depth + width)),
+            transcendentals=0,
+        ),
+        name="product",
+    )(grad_z, w_proj)
 
 
 def solution(mesh):

time: 35.2 us -> 35.2 us (level)
  matrix products: 2.87 us -> 0 us
  Pallas kernels: 32 us -> 33.9 us
  local copies, waits for them, and re-layouts: 0.01 us -> 0.95 us
    dot_general x1 -> x0, matrix products: 2.87 us -> none  [shards(): lax.dot_general(grad_z, w_proj, NT_DIMS, preferred_element_type=jnp.float32)]
    pallas_call x0 -> x1, Pallas kernels: none -> 1.92 us  [shards(): pl.pallas_call(product, out_shape=jax.ShapeDtypeStruct((group, depth), jn...]
    unnamed x2 -> x4, local copies, waits for them, and re-layouts: 0.01 us -> 0.95 us
where the time goes in v8:
time: 35.2 us; the launch traced here: 34.9 us
  Pallas kernels  33.9 us (96%)
  local copies, waits for them, and re-layouts  0.95 us (3%)
    pallas_call x1, Pallas kernels, shards(): pl.pallas_call(functools.partial(kernel, n_tensor, n_row, n_col, rates.sh...  32 us
    pallas_call x1, Pallas kernels, shards(): pl.pallas_call(product, out_shape=jax.ShapeDtypeStruct((group, depth), jn...  1.92 us
    unnamed x4, local copies, waits for them, and re-layouts  0.95 us

profile of v8, /device:TPU:1, one launch (start us, length us, event | category | flops | bytes accessed | tf_op | source)
XLA Modules:
  0.0 34.9 jit_solution(4289902417520118263)
XLA Ops:
  0.0 0.0 copy-start
  0.0 32.0 %mmd.1.grad_ref = bf16[128,1024]{1,0:T(8,128)(2,1)} custom-call(bf16[128,1536]{1,0:T(8,128)(2,1)} %f_hbm.1, bf16[1536,1024]{1,0:T(8,128)(2,1)} %w_ref.1, s32[1,128]{1,0:T(1,128)} %bitcast.1, f32[5]{0:T(128)} %rates_ref.1), custom_call_target="tpu_custom_call" | custom-call | flops 939524096 | bytes 3932160 | tf_op jit(solution)/shard_map/mmd/pallas_call | solution.py:235
  32.0 0.0 copy-done
  32.0 0.0 copy-start.1
  32.1 0.9 %copy-done.1 = bf16[128,1024]{1,0:T(8,128)(2,1)S(1)} copy-done((bf16[128,1024]{1,0:T(8,128)(2,1)S(1)}, bf16[128,1024]{1,0:T(8,128)(2,1)}, u32[]{:S(2)}) %copy-start.1) | copy-done | bytes 262168
  33.0 1.9 %product.1 = bf16[128,1536]{1,0:T(8,128)(2,1)} custom-call(bf16[128,1024]{1,0:T(8,128)(2,1)S(1)} %copy-done.1, bf16[1536,1024]{1,0:T(8,128)(2,1)S(1)} %copy-done), custom_call_target="tpu_custom_call" | custom-call | flops 402653184 | bytes 3801088 | tf_op jit(solution)/shard_map/product/pallas_call | solution.py:276
Async XLA Ops:
  0.0 32.0 %copy-start = (bf16[1536,1024]{1,0:T(8,128)(2,1)S(1)}, bf16[1536,1024]{1,0:T(8,128)(2,1)}, u32[]{:S(2)}) copy-start(bf16[1536,1024]{1,0:T(8,128)(2,1)} %w_ref.1) | copy-start | bytes 9437188
  32.0 1.0 %copy-start.1 = (bf16[128,1024]{1,0:T(8,128)(2,1)S(1)}, bf16[128,1024]{1,0:T(8,128)(2,1)}, u32[]{:S(2)}) copy-start(bf16[128,1024]{1,0:T(8,128)(2,1)} %mmd.1.grad_ref) | copy-start | bytes 786436
